TPU v7x, 32 devices: a whole 2x2x4 slice. The times are simulated.
32 devices in a mesh: crow: 8 (over z, x), ccol: 4 (over y, core).
Axes of the slice: x: 2, y: 2, z: 4, core: 2. Of those that a mesh axis runs over, the one named last changes fastest.
Arguments:
- sketch: float32 [131072, 512], P(('crow', 'ccol')), may hold values from -120 to 120, as said below
Outputs:
- posterior_basis: float32 [131072, 512], P(('crow', 'ccol'))
- mean_log_eigen: float32 [], replicated
Inputs may be any that keep to these rules, and one draw needn't show every extreme that they name: Entries of the sketch are real numbers of either sign.
All inputs are finite; a program needn't handle non-finite values.
Results may differ from a plain program's by a relative error of at most 0.0003.
Values sent between devices are 32-bit elements; how exact they have to be, the bound alone decides.
No kernel may reach another device: no remote copies, remote signals or barrier semaphores. Data moves between devices by JAX's collectives and lax.ppermute only.
A program may use at most 128 MiB of HBM per device.

v0:
```python
import math

import jax
import jax.numpy as jnp
from jax import lax
from jax.sharding import PartitionSpec as P


def on_device(sketch):
    rows_dev = sketch.shape[0]
    width = sketch.shape[1]
    rows_all = rows_dev * lax.axis_size("crow") * lax.axis_size("ccol")
    eye = jnp.eye(width, dtype=jnp.float32)
    partial_value = lax.dot_general(
        sketch,
        sketch,
        (((0,), (0,)), ((), ())),
        precision=lax.Precision.HIGHEST,
        preferred_element_type=jnp.float32,
    )
    summed = lax.psum(partial_value, ("crow", "ccol"))
    summed = summed + jnp.float32(rows_all) * eye
    factor = jnp.linalg.cholesky(summed)
    inverse = jax.scipy.linalg.cho_solve((factor, True), jnp.float32(rows_all) * eye)
    inverse = 0.5 * (inverse + inverse.T)
    posterior_basis = jnp.dot(
        sketch, inverse, precision=lax.Precision.HIGHEST, preferred_element_type=jnp.float32
    )
    logdet = 2.0 * jnp.sum(jnp.log(jnp.diagonal(factor))) - width * math.log(rows_all)
    return (posterior_basis, logdet / jnp.float32(width))


def solution(mesh):
    return jax.shard_map(
        on_device,
        mesh=mesh,
        in_specs=(P(("crow", "ccol"), None),),
        out_specs=(P(("crow", "ccol"), None), P()),
        check_vma=False,
    )
```

profile of v0, /device:TPU:0, one launch (start us, length us, event | category | flops | bytes accessed | tf_op | source)
XLA Modules:
  0.0 365.1 jit_solution(418210834424255626)
XLA Ops:
  7.2 18.5 %fusion.55 = f32[512,512]{0,1:T(8,128)} fusion(f32[4096,512]{1,0:T(8,128)} %param.1), kind=kOutput, calls=%fused_computation.99 | convolution fusion | flops 12884901888 | bytes 9437184 | tf_op jit(solution)/shard_map/dot_general | solution.py:14
  25.7 1.1 fusion.4
  26.8 131.6 %all-reduce.3.cloned.1.call-done = f32[512,512]{0,1:T(8,128)} async-done(((f32[512,512]{0,1:T(8,128)}), f32[512,512]{0,1:T(8,128)}) %all-reduce.3.cloned.1.call-update) | async-done | bytes 1048592 | tf_op jit(solution)/shard_map/psum | solution.py:21
  158.4 1.3 fusion.22
  159.8 0.3 copy.20
  160.1 1.5 fusion.2
  161.6 11.7 %cholesky.103 = f32[128,128]{1,0:T(8,128)S(1)} custom-call(f32[128,128]{1,0:T(8,128)S(1)} %cholesky.263), custom_call_target="Cholesky" | custom-call | tf_op jit(solution)/shard_map/jit(cholesky)/cholesky | solution.py:23
  173.3 0.1 copy.21
  173.5 9.8 %custom-call.34 = f32[1,128,128]{1,2,0:T(8,128)S(1)} custom-call(f32[1,128,128]{2,1,0:T(8,128)S(1)} %get-tuple-element.39), custom_call_target="InvertDiagBlocksLowerTriangular" | custom-call | tf_op jit(solution)/shard_map/jit(cholesky)/cholesky | solution.py:23
  183.3 0.3 fusion.29
  183.6 0.3 convolution_subtract_fusion.6
  183.9 0.1 copy.22
  184.1 11.7 %cholesky.215 = f32[128,128]{1,0:T(8,128)S(1)} custom-call(f32[128,128]{1,0:T(8,128)S(1)} %cholesky.267), custom_call_target="Cholesky" | custom-call | tf_op jit(solution)/shard_map/jit(cholesky)/cholesky | solution.py:23
  195.8 0.1 copy.23
  195.9 10.0 %custom-call.35 = f32[1,128,128]{1,2,0:T(8,128)S(1)} custom-call(f32[1,128,128]{2,1,0:T(8,128)S(1)} %get-tuple-element.37), custom_call_target="InvertDiagBlocksLowerTriangular" | custom-call | tf_op jit(solution)/shard_map/jit(cholesky)/cholesky | solution.py:23
  205.9 0.1 cholesky.222
  206.1 0.3 convolution_dynamic-update-slice_fusion
  206.4 0.6 convolution_subtract_fusion.7
  207.0 11.7 %cholesky.236 = f32[128,128]{1,0:T(8,128)S(1)} custom-call(f32[128,128]{1,0:T(8,128)S(1)} %cholesky.272), custom_call_target="Cholesky" | custom-call | tf_op jit(solution)/shard_map/jit(cholesky)/cholesky | solution.py:23
  218.7 0.1 copy.25
  218.9 9.8 %custom-call.36 = f32[1,128,128]{1,2,0:T(8,128)S(1)} custom-call(f32[1,128,128]{2,1,0:T(8,128)S(1)} %get-tuple-element.35), custom_call_target="InvertDiagBlocksLowerTriangular" | custom-call | tf_op jit(solution)/shard_map/jit(cholesky)/cholesky | solution.py:23
  228.7 0.3 convolution_dynamic-update-slice_fusion.1
  229.0 0.5 convolution_subtract_fusion.8
  229.5 12.1 %cholesky.253 = f32[128,128]{1,0:T(8,128)S(1)} custom-call(f32[128,128]{1,0:T(8,128)S(1)} %convolution_subtract_fusion.8), custom_call_target="Cholesky" | custom-call | tf_op jit(solution)/shard_map/jit(cholesky)/cholesky | solution.py:23
  241.7 0.7 compare_reduce_fusion.1
  242.5 0.6 compare_reduce_fusion
  243.1 0.7 compare_reduce_fusion.2
  246.3 0.3 fusion.3
  246.6 11.0 %while.1 = (s32[]{:T(128)}, f32[512,512]{0,1:T(8,128)S(1)}, s32[4,2]{0,1:T(2,128)S(1)}, f32[4,128,128]{2,1,0:T(8,128)}, s32[]{:T(128)}) while((s32[]{:T(128)}, f32[512,512]{0,1:T(8,128)S(1)}, s32[4,2]{0,1:T(2,128)S(1)}, f32[4,128,128]{2,1,0:T(8,128)}, s32[]{:T(128)}) %tuple.32), condition=%wide.while_cond, body=%wide.while_body.sunk | while | flops 2 | bytes 393329 | solution.py:24
  246.7 0.6 fusion.70
  247.3 1.3 dynamic-slice.7
  248.7 0.6 bitcast_dynamic-update-slice_fusion.2
  249.4 0.6 fusion.70
  250.0 1.3 dynamic-slice.7
  251.5 0.6 bitcast_dynamic-update-slice_fusion.2
  252.2 0.6 fusion.70
  252.8 1.3 dynamic-slice.7
  254.2 0.6 bitcast_dynamic-update-slice_fusion.2
  254.9 0.6 fusion.70
  255.5 1.3 dynamic-slice.7
  256.9 0.6 bitcast_dynamic-update-slice_fusion.2
  257.6 40.1 %custom-call.37 = f32[4,128,128]{1,2,0:T(8,128)S(1)} custom-call(f32[4,128,128]{2,1,0:T(8,128)} %get-tuple-element.9), custom_call_target="InvertDiagBlocksLowerTriangular" | custom-call | tf_op jit(solution)/shard_map/jit(_cho_solve)/triangular_solve | solution.py:24
  297.7 1.4 fusion.23
  299.1 1.5 convolution_subtract_fusion.3
  300.6 0.4 fusion.44
  301.1 2.0 convolution_subtract_fusion.2
  303.0 0.4 fusion.46
  303.4 2.4 convolution_subtract_fusion.5
  305.9 0.4 fusion.48
  306.3 0.4 fusion.47
  306.7 0.4 convolution_subtract_fusion.1
  307.1 0.4 fusion.45
  307.4 0.4 convolution_subtract_fusion
  307.9 0.4 fusion.43
  308.2 1.3 convolution_subtract_fusion.4
  309.6 0.1 copy.30
  309.7 0.1 copy.31
  309.9 0.1 copy.32
  310.0 4.5 %gather_fusion = f32[512]{0:T(512)S(1)} fusion(f32[512,512]{0,1:T(8,128)S(1)} %get-tuple-element.31, s32[512]{0:T(512)S(1)} %bitcast.66), kind=kCustom, calls=%fused_computation | custom fusion | bytes 8192 | tf_op jit(solution)/shard_map/jit(diagonal)/cond/branch_0_fun/gather | solution.py:29
  314.5 0.6 log_reduce_fusion
  315.1 1.5 fusion.42
  316.8 0.3 copy.33
  317.1 30.2 %convolution_bitcast_fusion = f32[4096,512]{0,1:T(8,128)} fusion(f32[4096,512]{1,0:T(8,128)} %param.1, f32[512,512]{1,0:T(8,128)S(1)} %copy.33, f32[128,512]{0,1:T(8,128)S(1)} %copy.32, f32[128,512]{0,1:T(8,128)S(1)} %copy.31, f32[128,512]{0,1:T(8,128)S(1)} %copy.30, f32[128,512]{0,1:T(8,128)S(1)} %fusion.42), kind=kOutput, calls=%fused_computation.3 | convolution fusion | flops 12886212608 | bytes 18874368 | tf_op jit(solution)/shard_map/dot_general | solution.py:26
  347.4 8.9 %copy.34 = f32[4096,512]{1,0:T(8,128)} copy(f32[4096,512]{0,1:T(8,128)} %convolution_bitcast_fusion) | data formatting | bytes 16777216
  (27 shorter events, 1.1 us)
Async XLA Ops:
  7.2 151.3 %all-reduce.3.cloned.1.call-start = ((), (), s32[]{:S(2)}) async-start(), calls=%async_computation | async-start | bytes 2097152 | tf_op jit(solution)/shard_map/psum | solution.py:21
Sparse Core Ops, SparseCore 0:
  25.8 132.5 all-reduce.2
where the time goes:
time: 369 us; the launch traced here: 365 us
  waiting for transfers between devices  132 us (36%)
  other arithmetic  124 us (34%)
  matrix products  64.4 us (17%)
  local copies, waits for them, and re-layouts  26.1 us (7%)
  between operations  18.9 us (5%)
    psum x1, waiting for transfers between devices, on_device(): summed = lax.psum(partial_value, ('crow', 'ccol'))  132 us
    another operation x14, other arithmetic, on_device(): factor = jnp.linalg.cholesky(summed)  79 us
    another operation x4, other arithmetic, on_device(): jax.scipy.linalg.cho_solve((factor, True), jnp.float32(rows_all) * eye)  40.4 us
    dot_general x1, matrix products, on_device(): jnp.dot(sketch, inverse, precision=lax.Precision.HIGHEST, preferred_eleme...  30.2 us
    dot_general x1, matrix products, on_device(): lax.dot_general(sketch, sketch, (((0,), (0,)), ((), ())), precision=lax.P...  18.5 us
    another operation x14, matrix products, on_device(): jax.scipy.linalg.cho_solve((factor, True), jnp.float32(rows_all) * eye)  13.3 us
    another operation x20, local copies, waits for them, and re-layouts  10.9 us
    unnamed x1, local copies, waits for them, and re-layouts  8.94 us
  transfers between devices with their start and end apart: 1, of which 1 were waited for; matrix products, arithmetic and copies ran while one was open for 0% of the time, Pallas kernels for 0%

commit v1 on v0

v1 whole, which is shorter than its diff:
```python
import functools

import jax
import jax.numpy as jnp
from jax import lax
from jax.experimental import pallas as pl
from jax.experimental.pallas import tpu as pltpu
from jax.sharding import PartitionSpec as P

AXES = ("crow", "ccol")
TILE = 128
F32 = jnp.float32
BF16 = jnp.bfloat16
LOG1P = {
    1: 0.9999739192217169,
    2: -0.49928683013429037,
    3: 0.32664225835205063,
    4: -0.21934280863425915,
    5: 0.12031934947180563,
    6: -0.037875575885947615,
    8: 0.0027171687390490683,
}
MAX_SQUARINGS = 12
VMEM_LIMIT = 48 * 1024 * 1024


def split(x):
    high = x.astype(BF16)
    return high, (x - high.astype(F32)).astype(BF16)


def split3(x):
    high = x.astype(BF16)
    rest = x - high.astype(F32)
    middle = rest.astype(BF16)
    return high, middle, (rest - middle.astype(F32)).astype(BF16)


def multiply(acc, left, staged=None):
    pltpu.matmul_acc_lhs(acc, left, load_staged_rhs=staged)


def sums_of(*units):
    for unit, terms in enumerate(units):
        for t, (tile, _) in enumerate(terms[:2]):
            pltpu.matmul_push_rhs(tile, t, unit)
    for t in range(max(len(terms) for terms in units)):
        for unit, terms in enumerate(units):
            if t < len(terms):
                for n, (acc, left) in enumerate(terms[t][1]):
                    multiply(acc, left, t % 2 if n == 0 else None)
                if t + 2 < len(terms):
                    pltpu.matmul_push_rhs(terms[t + 2][0], t % 2, unit)


def pop_both(one, two):
    return pltpu.matmul_pop(one) + pltpu.matmul_pop(two)


def dot6(accs, a, b):
    one, two = accs[:2]
    a0, a1, a2 = split3(a)
    b0, b1, b2 = split3(b)
    sums_of(
        [(b0, [(one, a0), (one, a1), (one, a2)])],
        [(b1, [(two, a0), (two, a1)]), (b2, [(two, a0)])],
    )
    return pop_both(one, two)


def eye_mask(n):
    return lax.broadcasted_iota(jnp.int32, (n, n), 0) == lax.broadcasted_iota(jnp.int32, (n, n), 1)


def above_mask(n):
    return lax.broadcasted_iota(jnp.int32, (n, n), 0) < lax.broadcasted_iota(jnp.int32, (n, n), 1)


class Plan:
    def __init__(self, nrow, ncol, width):
        self.ncol = ncol
        self.n = nrow * ncol
        self.parts = self.n // 4
        bits = [1 << b for b in range(1, self.n.bit_length() - 1)]
        y = [b for b in bits if b < ncol]
        x = [b for b in bits if ncol <= b < self.parts]
        self.z = [b for b in bits if b >= self.parts]
        self.stages = list(zip(x, y))
        tiles = width // TILE
        self.pairs = [(i, j) for i in range(tiles) for j in range(i + 1, tiles)]
        self.folds = [(i, i + 1) for i in range(0, tiles, 2)]
        self.diagonals = (len(self.pairs) + len(self.folds)) * TILE
        self.chunk = 8 * pl.cdiv(self.diagonals + 8, 8 * self.parts)
        self.half = self.chunk * self.parts // 2

    def me(self):
        return lax.axis_index("crow") * self.ncol + lax.axis_index("ccol")

    def rows(self, part, me):
        order = 0
        for mask in sum(self.stages, ()):
            here = jnp.bitwise_and(jnp.bitwise_xor(part, me), mask) // mask
            order = 2 * order + here
        return pl.ds(pl.multiple_of(order * self.chunk, 8), self.chunk)

    def halves(self, me, copy):
        for core in range(2):

            @pl.when(jnp.bitwise_and(me, 1) == core)
            def _():
                for part in range(self.parts):
                    copy(part, part & 1 == core)

    def swap(self, x, mask):
        return lax.ppermute(x, AXES, [(i, i ^ mask) for i in range(self.n)])


def gram_kernel(
    plan, sketch_ref, keep_ref, send_ref,
    rows_ref, flat, turned, whole, packed, load_sem,
):
    blocks = load_sem.shape[0]
    size = rows_ref.shape[0] // blocks
    width = rows_ref.shape[1]
    half = width // 2
    first, second = slice(0, half), slice(half, width)

    def load(i):
        at = pl.ds(i * size, size)
        return pltpu.make_async_copy(sketch_ref.at[at], rows_ref.at[at], load_sem.at[i])

    def prepare(i):
        load(i).wait()
        h, l = split(rows_ref[i * size : (i + 1) * size, :])
        flat[2 * (i % 2)] = h
        flat[2 * (i % 2) + 1] = l
        turned[2 * (i % 2)] = h.T
        turned[2 * (i % 2) + 1] = l.T

    def push(slot, staged):
        pltpu.matmul_push_rhs(flat[slot, :, first], staged, 0)
        pltpu.matmul_push_rhs(flat[slot, :, second], staged, 1)

    for i in range(blocks):
        load(i).start()
    prepare(0)

    def sums(s00, z10, c00, z01, s11, c11):
        push(0, 0)
        for i in range(blocks):
            h, l = 2 * (i % 2), 2 * (i % 2) + 1
            push(l, 1)
            multiply(s00, turned[h, first, :], 0)
            multiply(s11, turned[h, second, :], 0)
            multiply(z10, turned[h, second, :])
            if i + 1 < blocks:
                prepare(i + 1)
                push(2 * ((i + 1) % 2), 0)
            multiply(s00, turned[l, first, :], 1)
            multiply(z01, turned[l, first, :], 1)
            multiply(c00, turned[h, first, :])
            multiply(z01, turned[h, first, :])
            multiply(z10, turned[h, second, :])
            multiply(s11, turned[l, second, :])
            multiply(c11, turned[h, second, :])

        cross = pltpu.matmul_pop(c00)
        whole[first, first] = pltpu.matmul_pop(s00) + cross + cross.T
        whole[first, second] = pltpu.matmul_pop(z01) + pltpu.matmul_pop(z10).T
        cross = pltpu.matmul_pop(c11)
        whole[second, second] = pltpu.matmul_pop(s11) + cross + cross.T

    square = (half, half)
    units = (0, 0, 0, 1, 1, 1)
    pl.run_scoped(sums, *[pltpu.ACC(unit)(square, F32) for unit in units])
    tile = lambda i, j: whole[i * TILE : (i + 1) * TILE, j * TILE : (j + 1) * TILE]
    packed[plan.diagonals :, :] = jnp.zeros_like(packed[plan.diagonals :, :])
    for t, (i, j) in enumerate(plan.pairs):
        packed[t * TILE : (t + 1) * TILE, :] = tile(i, j)
    for f, (i, j) in enumerate(plan.folds):
        t = len(plan.pairs) + f
        packed[t * TILE : (t + 1) * TILE, :] = jnp.where(above_mask(TILE), tile(i, i), tile(j, j))
        line = jnp.sum(jnp.where(eye_mask(TILE), tile(i, i), 0.0), axis=0, keepdims=True)
        packed[plan.diagonals + f : plan.diagonals + f + 1, :] = line
    me = plan.me()

    def copy(part, own):
        ref = keep_ref if own else send_ref
        ref[plan.rows(part, me), :] = packed[part * plan.chunk : (part + 1) * plan.chunk, :]

    plan.halves(me, copy)


def gram(plan, sketch):
    rows, width = sketch.shape
    half = width // 2
    return pl.pallas_call(
        functools.partial(gram_kernel, plan),
        in_specs=[pl.BlockSpec(memory_space=pl.ANY)],
        out_specs=[pl.BlockSpec(memory_space=pltpu.VMEM)] * 2,
        out_shape=[jax.ShapeDtypeStruct((plan.half, TILE), F32)] * 2,
        scratch_shapes=[
            pltpu.VMEM((rows, width), F32),
            pltpu.VMEM((4, half, width), BF16),
            pltpu.VMEM((4, width, half), BF16),
            pltpu.VMEM((width, width), F32),
            pltpu.VMEM((2 * plan.half, TILE), F32),
            pltpu.SemaphoreType.DMA((rows // half,)),
        ],
        compiler_params=pltpu.CompilerParams(vmem_limit_bytes=VMEM_LIMIT),
    )(sketch)


def share(plan, keep, send):
    own = keep + plan.swap(send, 1)
    for x, y in plan.stages:
        m = own.shape[0] // 4
        got = [plan.swap(own[d * m : (d + 1) * m], k) for d, k in ((1, y), (2, x), (3, x + y))]
        own = own[:m] + got[0] + got[1] + got[2]
    for z in plan.z:
        own = own + plan.swap(own, z)
    for x, y in reversed(plan.stages):
        own = jnp.concatenate([own] + [plan.swap(own, k) for k in (y, x, x + y)], axis=0)
    return own, plan.swap(own, 1)


def fold(x):
    n = x.shape[0]
    return jnp.sum(x.reshape(n // 8, 8, x.shape[1]), axis=0)


def near_inverse(accs, a, o_ref, y_ref, acc_ref):
    n = a.shape[0]
    eye = eye_mask(n)
    diagonal = jnp.where(eye, a, 0.0)
    s_row = lax.rsqrt(jnp.sum(diagonal, axis=0, keepdims=True))
    s_col = lax.rsqrt(jnp.sum(diagonal, axis=1, keepdims=True))
    c = a * s_col * s_row
    norm = jnp.max(jnp.sum(jnp.abs(c), axis=0, keepdims=True), axis=1, keepdims=True)
    inv_norm = 1.0 / norm
    rho0 = 1.0 - inv_norm
    start = jnp.where(eye, 1.0 - rho0, 0.0) - c * inv_norm
    zero = jnp.zeros((n, n), F32)
    o_ref[0] = start
    o_ref[1] = zero
    o_ref[2] = zero
    y_ref[...] = zero
    acc_ref[...] = fold(jnp.where(eye, LOG1P[1] * (start + rho0), 0.0))
    square0, square1, factor0, factor1 = accs

    def more(carry):
        return jnp.logical_and(carry[0] < MAX_SQUARINGS, carry[1] >= 1e-3)

    def body(carry):
        k, _, rho, rho1, rho2, xi = carry
        o = o_ref[k % 3]
        y = y_ref[...]
        oh, ol = split(o)
        yh, yl = split(y)
        sums_of(
            [(oh, [(square0, oh), (square0, ol), (factor0, yh)])],
            [(oh, [(factor1, yl)]), (ol, [(square1, oh), (factor1, yh)])],
        )
        o1 = o_ref[(k + 2) % 3]
        o2 = o_ref[(k + 1) % 3]
        w0 = LOG1P[1] + LOG1P[2] + jnp.where(k >= 1, LOG1P[4], 0.0) + jnp.where(k >= 2, LOG1P[8], 0.0)
        w1 = jnp.where(k >= 1, LOG1P[3], 0.0) + jnp.where(k >= 2, LOG1P[6], 0.0)
        w2 = LOG1P[5]
        r = o + jnp.where(eye, rho, 0.0)
        mixed = w0 * o + w1 * o1 + w2 * o2 + jnp.where(eye, w0 * rho + w1 * rho1 + w2 * rho2, 0.0)
        acc_ref[...] += fold(r * mixed)
        size = jnp.sum(fold(r * r))
        o_ref[(k + 1) % 3] = (2.0 * rho) * o + pop_both(square0, square1)
        y_ref[...] = (1.0 + rho) * y + xi * o + pop_both(factor0, factor1)
        return k + 1, size, rho * rho, rho, rho1, xi * (1.0 + rho)

    none = jnp.float32(0.0)
    begin = (jnp.int32(0), jnp.float32(1e30), jnp.max(rho0), none, none, jnp.max(inv_norm))
    _, size, _, _, _, xi = lax.while_loop(more, body, begin)
    x = y_ref[...] + jnp.where(eye, xi, 0.0)
    rest = jnp.where(eye, 1.0, 0.0) - dot6(accs, c, x)
    sums_of([(rest.astype(BF16), [(square0, x.astype(BF16))])])
    x = x + pltpu.matmul_pop(square0)
    log_det = n * jnp.log(norm) - jnp.sum(acc_ref[...], keepdims=True) - 2.0 * jnp.sum(
        jnp.log(s_row), axis=1, keepdims=True
    )
    return x * s_col * s_row, log_det, size


def sweep(a_ref, c_ref, log_ref):
    n = a_ref.shape[0]
    eye = eye_mask(n)
    diagonal = jnp.where(eye, a_ref[...], 0.0)
    s_row = lax.rsqrt(jnp.sum(diagonal, axis=0, keepdims=True))
    s_col = lax.rsqrt(jnp.sum(diagonal, axis=1, keepdims=True))
    c_ref[...] = a_ref[...] * s_col * s_row
    log_ref[...] = -2.0 * jnp.sum(jnp.log(s_row), axis=1, keepdims=True)
    lane = lax.broadcasted_iota(jnp.int32, (1, n), 1)

    @pl.loop(0, n)
    def _(k):
        row = c_ref[pl.ds(k, 1), :]
        here = lane == k
        pivot = jnp.sum(jnp.where(here, row, 0.0), axis=1, keepdims=True)
        log_ref[...] += jnp.log(pivot)
        u = jnp.where(here, pivot - 1.0, row)
        column = jnp.broadcast_to(u, (8, n)).T[:, :1]
        outer = column * (u / pivot)
        c_ref[...] = c_ref[...] - outer
        c_ref[pl.ds(k, 1), :] = c_ref[pl.ds(k, 1), :] - jnp.where(here, 2.0, 0.0)

    c_ref[...] = -(c_ref[...] * s_col * s_row)


def solve_kernel(
    plan, rows_all, near_ref, far_ref, sketch_ref, out_ref, log_ref,
    packed, a_ref, x_ref, o_ref, y_ref, acc_ref,
    rows_ref, result, mats, parts, load_sem, store_sem,
):
    blocks = load_sem.shape[0]
    size = rows_ref.shape[0] // blocks

    def load(i):
        at = pl.ds(i * size, size)
        return pltpu.make_async_copy(sketch_ref.at[at], rows_ref.at[at], load_sem.at[i])

    def store(i):
        at = pl.ds(i * size, size)
        return pltpu.make_async_copy(result.at[at], out_ref.at[at], store_sem.at[i])

    for i in range(blocks):
        load(i).start()

    n = a_ref.shape[0]
    m = n // 2
    me = plan.me()

    def copy(part, own):
        ref = near_ref if own else far_ref
        packed[part * plan.chunk : (part + 1) * plan.chunk, :] = ref[plan.rows(part, me), :]

    plan.halves(me, copy)

    scale = jnp.float32(1.0 / rows_all)
    unit = jnp.where(eye_mask(TILE), 1.0, 0.0)
    rows = lambda i: slice(i * TILE, (i + 1) * TILE)
    for t, (i, j) in enumerate(plan.pairs):
        tile = packed[rows(t), :] * scale
        a_ref[rows(i), rows(j)] = tile
        a_ref[rows(j), rows(i)] = tile.T
    above = above_mask(TILE)
    for f, (i, j) in enumerate(plan.folds):
        tile = packed[rows(len(plan.pairs) + f), :] * scale
        line = packed[plan.diagonals + f : plan.diagonals + f + 1, :] * scale
        mixed = jnp.where(eye_mask(TILE), line, jnp.where(above, tile, tile.T))
        a_ref[rows(i), rows(i)] = mixed + unit
        a_ref[rows(j), rows(j)] = jnp.where(above, tile.T, tile) + unit

    bufs = (o_ref, y_ref, acc_ref)

    def invert(*accs):
        x11, log1, size1 = near_inverse(accs, a_ref[:m, :m], *bufs)
        t12 = dot6(accs, x11, a_ref[:m, m:])
        schur = a_ref[m:, m:] - dot6(accs, a_ref[m:, :m], t12)
        x_ref[:m, :m] = x11
        x_ref[:m, m:] = t12
        x22, log2, size2 = near_inverse(accs, schur, *bufs)
        t12 = x_ref[:m, m:]
        x12 = -dot6(accs, t12, x22)
        x_ref[:m, :m] = x_ref[:m, :m] - dot6(accs, x12, t12.T)
        x_ref[:m, m:] = x12
        x_ref[m:, :m] = x12.T
        x_ref[m:, m:] = x22
        log_ref[...] = log1 + log2
        good = jnp.logical_and(size1 < 1e-3, size2 < 1e-3)

        @pl.when(jnp.logical_not(good))
        def _():
            sweep(a_ref, x_ref, log_ref)

    pl.run_scoped(invert, *[pltpu.ACC(unit)((m, m), F32) for unit in (0, 1, 0, 1)])
    log_ref[...] = log_ref[...] / n
    eye = eye_mask(n)
    diagonal = jnp.sum(jnp.where(eye, x_ref[...], 0.0), axis=0, keepdims=True)
    high, low = split(jnp.where(eye, 0.0, x_ref[...]))
    mats[0] = high
    mats[1] = low
    for i in range(blocks):
        load(i).wait()

    def prepare(i):
        h, l = split(rows_ref[i * size : (i + 1) * size, :])
        parts[2 * (i % 2)] = h
        parts[2 * (i % 2) + 1] = l

    steps = [(i, k, which) for i in range(blocks) for k in range(2) for which in range(2)]

    def push(step):
        _, k, which = steps[step]
        for unit in range(2):
            tile = mats[which, k * m : (k + 1) * m, unit * m : (unit + 1) * m]
            pltpu.matmul_push_rhs(tile, which, unit)

    def products(*accs):
        push(0)
        push(1)
        prepare(0)
        for step, (i, k, which) in enumerate(steps):
            h, l = 2 * (i % 2), 2 * (i % 2) + 1
            mine = accs[h : h + 2]
            cols = slice(k * m, (k + 1) * m)
            for acc in mine:
                multiply(acc, parts[h, :, cols], which)
            if which == 0:
                for acc in mine:
                    multiply(acc, parts[l, :, cols])
            if step + 2 < len(steps):
                push(step + 2)
            if k == 0 and which == 1 and i + 1 < blocks:
                prepare(i + 1)
            if k == 1 and which == 1:
                at = slice(i * size, (i + 1) * size)
                for unit, acc in enumerate(mine):
                    cols = slice(unit * m, (unit + 1) * m)
                    result[at, cols] = rows_ref[at, cols] * diagonal[:, cols] + pltpu.matmul_pop(acc)
                store(i).start()

    pl.run_scoped(products, *[pltpu.ACC(unit)((size, m), F32) for unit in (0, 1, 0, 1)])
    for i in range(blocks):
        store(i).wait()


def solve(plan, sketch, near, far):
    rows, width = sketch.shape
    m = width // 2
    block = min(512, rows)
    vmem = pl.BlockSpec(memory_space=pltpu.VMEM)
    hbm = pl.BlockSpec(memory_space=pl.ANY)
    return pl.pallas_call(
        functools.partial(solve_kernel, plan, rows * plan.n),
        in_specs=[vmem, vmem, hbm],
        out_specs=[hbm, vmem],
        out_shape=[
            jax.ShapeDtypeStruct((rows, width), F32),
            jax.ShapeDtypeStruct((1, 1), F32),
        ],
        scratch_shapes=[
            pltpu.VMEM((2 * plan.half, TILE), F32),
            pltpu.VMEM((width, width), F32),
            pltpu.VMEM((width, width), F32),
            pltpu.VMEM((3, m, m), F32),
            pltpu.VMEM((m, m), F32),
            pltpu.VMEM((8, m), F32),
            pltpu.VMEM((rows, width), F32),
            pltpu.VMEM((rows, width), F32),
            pltpu.VMEM((2, width, width), BF16),
            pltpu.VMEM((4, block, width), BF16),
            pltpu.SemaphoreType.DMA((rows // block,)),
            pltpu.SemaphoreType.DMA((rows // block,)),
        ],
        compiler_params=pltpu.CompilerParams(vmem_limit_bytes=VMEM_LIMIT),
    )(near, far, sketch)


def solution(mesh):
    nrow, ncol = mesh.shape["crow"], mesh.shape["ccol"]

    def on_device(sketch):
        plan = Plan(nrow, ncol, sketch.shape[1])
        keep, send = gram(plan, sketch)
        near, far = share(plan, keep, send)
        basis, log_mean = solve(plan, sketch, near, far)
        return basis, log_mean[0, 0]

    return jax.shard_map(
        on_device,
        mesh=mesh,
        in_specs=(P(AXES, None),),
        out_specs=(P(AXES, None), P()),
        check_vma=False,
    )
```

time: 369 us -> 247 us (0.67); the launches traced: 365 us -> 247 us
  Pallas kernels: 0 us -> 217 us
  other arithmetic: 124 us -> 0.1 us
  waiting for transfers between devices: 132 us -> 16.1 us
  matrix products: 64.4 us -> 0 us
  local copies, waits for them, and re-layouts: 26.1 us -> 0.02 us
  between operations: 18.9 us -> 0.83 us
  starting transfers between devices: 0.04 us -> 12.9 us
    pallas_call x0 -> x2, Pallas kernels: none -> 217 us  [the longest x1 210 us: solve(): pl.pallas_call(functools.partial(solve_kernel, plan, rows * plan.n), in_s...]
    psum x1 -> x0, waiting for transfers between devices: 132 us -> none  [on_device(): summed = lax.psum(partial_value, ('crow', 'ccol'))]
    another operation x18 -> x0, other arithmetic: 119 us -> none  [the longest x14 79 us: on_device(): factor = jnp.linalg.cholesky(summed)]
    dot_general x2 -> x0, matrix products: 48.7 us -> none  [the longest x1 30.2 us: on_device(): jnp.dot(sketch, inverse, precision=lax.Precision.HIGHEST, preferred_eleme...]
    ppermute x0 -> x10, waiting for transfers between devices: none -> 16.1 us  [swap(): return lax.ppermute(x, AXES, [(i, i ^ mask) for i in range(self.n)])]
    another operation x20 -> x0, matrix products: 15.7 us -> none  [the longest x14 13.3 us: on_device(): jax.scipy.linalg.cho_solve((factor, True), jnp.float32(rows_all) * eye)]
    ppermute x0 -> x10, starting transfers between devices: none -> 12.9 us  [swap(): return lax.ppermute(x, AXES, [(i, i ^ mask) for i in range(self.n)])]
    another operation x38 -> x0, local copies, waits for them, and re-layouts: 12.3 us -> none
  transfers between devices with their start and end apart: 1 -> 10, of which waited for: 1 -> 9; matrix products, arithmetic and copies ran while one was open for 0% -> 0% of each run, Pallas kernels for 0% -> 0%
where the time goes in v1:
time: 247 us
  Pallas kernels  217 us (88%)
  waiting for transfers between devices  16.1 us (7%)
  starting transfers between devices  12.9 us (5%)
    pallas_call x1, Pallas kernels, solve(): pl.pallas_call(functools.partial(solve_kernel, plan, rows * plan.n), in_s...  210 us
    ppermute x10, waiting for transfers between devices, swap(): return lax.ppermute(x, AXES, [(i, i ^ mask) for i in range(self.n)])  16.1 us
    ppermute x10, starting transfers between devices, swap(): return lax.ppermute(x, AXES, [(i, i ^ mask) for i in range(self.n)])  12.9 us
    pallas_call x1, Pallas kernels, gram(): pl.pallas_call(functools.partial(gram_kernel, plan), in_specs=[pl.BlockSp...  7.12 us
  transfers between devices with their start and end apart: 10, of which 9 were waited for; matrix products, arithmetic and copies ran while one was open for 0% of the time, Pallas kernels for 0%

profile of v1, /device:TPU:0, one launch (start us, length us, event | category | flops | bytes accessed | tf_op | source)
XLA Modules:
  0.0 246.8 jit_solution(3984797078418344353)
XLA Ops:
  0.6 7.1 %shard_map.30 = (f32[544,128]{1,0:T(8,128)S(1)}, f32[544,128]{1,0:T(8,128)S(1)}) custom-call(f32[4096,512]{1,0:T(8,128)} %sketch_ref.3), custom_call_target="tpu_custom_call" | custom-call | tf_op jit(solution)/shard_map/pallas_call | solution.py:197
  7.8 0.5 collective-permute-start
  8.3 1.2 collective-permute-done
  9.5 2.9 %collective-permute-start.1 = (f32[136,128]{1,0:T(8,128)S(1)}, f32[136,128]{1,0:T(8,128)S(1)}, u32[]{:S(2)}, u32[]{:S(2)}) collective-permute-start(f32[136,128]{1,0:T(8,128)S(1)} %get-tuple-element.10), channel_id=1, source_target_pairs={{0,2},{1,3},{2,0},{3,1},{4,6},{5,7},{6,4},{7,5},{8,10},{9,11},{10,... | collective-permute-start | bytes 208904 | tf_op jit(solution)/shard_map/ppermute | solution.py:115
  12.5 1.4 collective-permute-start.3
  13.9 0.1 collective-permute-start.2
  14.0 1.8 collective-permute-done.1
  15.8 2.5 %collective-permute-done.3 = f32[136,128]{1,0:T(8,128)S(1)} collective-permute-done((f32[136,128]{1,0:T(8,128)S(1)}, f32[136,128]{1,0:T(8,128)S(1)}, u32[]{:S(2)}, u32[]{:S(2)}) %collective-permute-start.3) | collective-permute-done | bytes 69664 | tf_op jit(solution)/shard_map/ppermute | solution.py:115
  18.3 0.0 collective-permute-done.2
  18.4 1.6 collective-permute-start.4
  20.0 2.7 %collective-permute-done.4 = f32[136,128]{1,0:T(8,128)S(1)} collective-permute-done((f32[136,128]{1,0:T(8,128)S(1)}, f32[136,128]{1,0:T(8,128)S(1)}, u32[]{:S(2)}, u32[]{:S(2)}) %collective-permute-start.4) | collective-permute-done | bytes 69664 | tf_op jit(solution)/shard_map/ppermute | solution.py:115
  22.8 2.7 %collective-permute-start.5 = (f32[136,128]{1,0:T(8,128)S(1)}, f32[136,128]{1,0:T(8,128)S(1)}, u32[]{:S(2)}, u32[]{:S(2)}) collective-permute-start(f32[136,128]{1,0:T(8,128)S(1)} %add.22), channel_id=1, source_target_pairs={{0,16},{1,17},{2,18},{3,19},{4,20},{5,21},{6,22},{7,23},{8,24},{9,... | collective-permute-start | bytes 208904 | tf_op jit(solution)/shard_map/ppermute | solution.py:115
  25.4 2.6 %collective-permute-done.5 = f32[136,128]{1,0:T(8,128)S(1)} collective-permute-done((f32[136,128]{1,0:T(8,128)S(1)}, f32[136,128]{1,0:T(8,128)S(1)}, u32[]{:S(2)}, u32[]{:S(2)}) %collective-permute-start.5) | collective-permute-done | bytes 69664 | tf_op jit(solution)/shard_map/ppermute | solution.py:115
  28.0 2.0 collective-permute-start.8
  30.1 0.9 collective-permute-start.7
  31.0 0.6 collective-permute-start.6
  31.6 1.7 collective-permute-done.8
  33.3 1.1 collective-permute-done.7
  34.4 0.9 collective-permute-done.6
  35.3 0.1 collective-permute-start.9
  35.4 1.5 collective-permute-done.9.far_ref
  36.9 209.7 %shard_map.31 = (f32[4096,512]{1,0:T(8,128)}, f32[1,1]{1,0:T(1,128)}) custom-call(f32[544,128]{1,0:T(8,128)S(1)} %pad_maximum_fusion.near_ref, f32[544,128]{1,0:T(8,128)S(1)} %collective-permute-done.9.far_ref, f32[4096,512]{1,0:T(8,128)} %sketch_ref.3), custom_call_target="tpu_custom_call" | custom-call | tf_op jit(solution)/shard_map/pallas_call | solution.py:439
  (6 shorter events, 0.1 us)
Async XLA Ops:
  7.8 1.7 collective-permute-start
  9.5 6.3 %collective-permute-start.1 = (f32[136,128]{1,0:T(8,128)S(1)}, f32[136,128]{1,0:T(8,128)S(1)}, u32[]{:S(2)}, u32[]{:S(2)}) collective-permute-start(f32[136,128]{1,0:T(8,128)S(1)} %get-tuple-element.10), channel_id=1, source_target_pairs={{0,2},{1,3},{2,0},{3,1},{4,6},{5,7},{6,4},{7,5},{8,10},{9,11},{10,... | collective-permute-start | bytes 208904 | tf_op jit(solution)/shard_map/ppermute | solution.py:115
  12.5 5.9 %collective-permute-start.3 = (f32[136,128]{1,0:T(8,128)S(1)}, f32[136,128]{1,0:T(8,128)S(1)}, u32[]{:S(2)}, u32[]{:S(2)}) collective-permute-start(f32[136,128]{1,0:T(8,128)S(1)} %get-tuple-element.11), channel_id=1, source_target_pairs={{0,6},{1,7},{2,4},{3,5},{4,2},{5,3},{6,0},{7,1},{8,14},{9,15},{10,... | collective-permute-start | bytes 208904 | tf_op jit(solution)/shard_map/ppermute | solution.py:115
  13.9 4.4 %collective-permute-start.2 = (f32[136,128]{1,0:T(8,128)S(1)}, f32[136,128]{1,0:T(8,128)S(1)}, u32[]{:S(2)}, u32[]{:S(2)}) collective-permute-start(f32[136,128]{1,0:T(8,128)S(1)} %get-tuple-element.12), channel_id=1, source_target_pairs={{0,4},{1,5},{2,6},{3,7},{4,0},{5,1},{6,2},{7,3},{8,12},{9,13},{10,... | collective-permute-start | bytes 208904 | tf_op jit(solution)/shard_map/ppermute | solution.py:115
  18.4 4.4 %collective-permute-start.4 = (f32[136,128]{1,0:T(8,128)S(1)}, f32[136,128]{1,0:T(8,128)S(1)}, u32[]{:S(2)}, u32[]{:S(2)}) collective-permute-start(f32[136,128]{1,0:T(8,128)S(1)} %fusion.1), channel_id=1, source_target_pairs={{0,8},{1,9},{2,10},{3,11},{4,12},{5,13},{6,14},{7,15},{8,0},{9,1},... | collective-permute-start | bytes 208904 | tf_op jit(solution)/shard_map/ppermute | solution.py:115
  22.8 5.3 %collective-permute-start.5 = (f32[136,128]{1,0:T(8,128)S(1)}, f32[136,128]{1,0:T(8,128)S(1)}, u32[]{:S(2)}, u32[]{:S(2)}) collective-permute-start(f32[136,128]{1,0:T(8,128)S(1)} %add.22), channel_id=1, source_target_pairs={{0,16},{1,17},{2,18},{3,19},{4,20},{5,21},{6,22},{7,23},{8,24},{9,... | collective-permute-start | bytes 208904 | tf_op jit(solution)/shard_map/ppermute | solution.py:115
  28.0 5.3 %collective-permute-start.8 = (f32[136,128]{1,0:T(8,128)S(1)}, f32[136,128]{1,0:T(8,128)S(1)}, u32[]{:S(2)}, u32[]{:S(2)}) collective-permute-start(f32[136,128]{1,0:T(8,128)S(1)} %add.23), channel_id=1, source_target_pairs={{0,6},{1,7},{2,4},{3,5},{4,2},{5,3},{6,0},{7,1},{8,14},{9,15},{10,... | collective-permute-start | bytes 208904 | tf_op jit(solution)/shard_map/ppermute | solution.py:115
  30.1 4.3 %collective-permute-start.7 = (f32[136,128]{1,0:T(8,128)S(1)}, f32[136,128]{1,0:T(8,128)S(1)}, u32[]{:S(2)}, u32[]{:S(2)}) collective-permute-start(f32[136,128]{1,0:T(8,128)S(1)} %add.23), channel_id=1, source_target_pairs={{0,4},{1,5},{2,6},{3,7},{4,0},{5,1},{6,2},{7,3},{8,12},{9,13},{10,... | collective-permute-start | bytes 208904 | tf_op jit(solution)/shard_map/ppermute | solution.py:115
  31.0 4.3 %collective-permute-start.6 = (f32[136,128]{1,0:T(8,128)S(1)}, f32[136,128]{1,0:T(8,128)S(1)}, u32[]{:S(2)}, u32[]{:S(2)}) collective-permute-start(f32[136,128]{1,0:T(8,128)S(1)} %add.23), channel_id=1, source_target_pairs={{0,2},{1,3},{2,0},{3,1},{4,6},{5,7},{6,4},{7,5},{8,10},{9,11},{10,... | collective-permute-start | bytes 208904 | tf_op jit(solution)/shard_map/ppermute | solution.py:115
  35.3 1.6 collective-permute-start.9

commit v2 on v1

--- a/solution.py
+++ b/solution.py
@@ -217,8 +217,9 @@
         m = own.shape[0] // 4
         got = [plan.swap(own[d * m : (d + 1) * m], k) for d, k in ((1, y), (2, x), (3, x + y))]
         own = own[:m] + got[0] + got[1] + got[2]
-    for z in plan.z:
-        own = own + plan.swap(own, z)
+    one, two = plan.z
+    got = [plan.swap(own, z) for z in (one, two, one + two)]
+    own = (own + got[0]) + (got[1] + got[2])
     for x, y in reversed(plan.stages):
         own = jnp.concatenate([own] + [plan.swap(own, k) for k in (y, x, x + y)], axis=0)
     return own, plan.swap(own, 1)
@@ -229,7 +230,7 @@
     return jnp.sum(x.reshape(n // 8, 8, x.shape[1]), axis=0)
 
 
-def near_inverse(accs, a, o_ref, y_ref, acc_ref):
+def near_inverse(accs, a, o_ref, y_ref, r1_ref, r2_ref, acc_ref):
     n = a.shape[0]
     eye = eye_mask(n)
     diagonal = jnp.where(eye, a, 0.0)
@@ -240,11 +241,9 @@
     inv_norm = 1.0 / norm
     rho0 = 1.0 - inv_norm
     start = jnp.where(eye, 1.0 - rho0, 0.0) - c * inv_norm
-    zero = jnp.zeros((n, n), F32)
-    o_ref[0] = start
-    o_ref[1] = zero
-    o_ref[2] = zero
-    y_ref[...] = zero
+    o_ref[...] = start
+    for ref in (y_ref, r1_ref, r2_ref):
+        ref[...] = jnp.zeros((n, n), F32)
     acc_ref[...] = fold(jnp.where(eye, LOG1P[1] * (start + rho0), 0.0))
     square0, square1, factor0, factor1 = accs
 
@@ -252,31 +251,29 @@
         return jnp.logical_and(carry[0] < MAX_SQUARINGS, carry[1] >= 1e-3)
 
     def body(carry):
-        k, _, rho, rho1, rho2, xi = carry
-        o = o_ref[k % 3]
+        k, _, rho, xi = carry
+        o = o_ref[...]
         y = y_ref[...]
         oh, ol = split(o)
         yh, yl = split(y)
         sums_of(
             [(oh, [(square0, oh), (square0, ol), (factor0, yh)])],
-            [(oh, [(factor1, yl)]), (ol, [(square1, oh), (factor1, yh)])],
+            [(ol, [(square1, oh), (factor1, yh)]), (oh, [(factor1, yl)])],
         )
-        o1 = o_ref[(k + 2) % 3]
-        o2 = o_ref[(k + 1) % 3]
+        r1 = r1_ref[...]
+        r = o + jnp.where(eye, rho, 0.0)
         w0 = LOG1P[1] + LOG1P[2] + jnp.where(k >= 1, LOG1P[4], 0.0) + jnp.where(k >= 2, LOG1P[8], 0.0)
         w1 = jnp.where(k >= 1, LOG1P[3], 0.0) + jnp.where(k >= 2, LOG1P[6], 0.0)
-        w2 = LOG1P[5]
-        r = o + jnp.where(eye, rho, 0.0)
-        mixed = w0 * o + w1 * o1 + w2 * o2 + jnp.where(eye, w0 * rho + w1 * rho1 + w2 * rho2, 0.0)
-        acc_ref[...] += fold(r * mixed)
+        acc_ref[...] += fold(r * (w0 * r + w1 * r1 + LOG1P[5] * r2_ref[...]))
         size = jnp.sum(fold(r * r))
-        o_ref[(k + 1) % 3] = (2.0 * rho) * o + pop_both(square0, square1)
+        r2_ref[...] = r1
+        r1_ref[...] = r
+        o_ref[...] = (2.0 * rho) * o + pop_both(square0, square1)
         y_ref[...] = (1.0 + rho) * y + xi * o + pop_both(factor0, factor1)
-        return k + 1, size, rho * rho, rho, rho1, xi * (1.0 + rho)
-
-    none = jnp.float32(0.0)
-    begin = (jnp.int32(0), jnp.float32(1e30), jnp.max(rho0), none, none, jnp.max(inv_norm))
-    _, size, _, _, _, xi = lax.while_loop(more, body, begin)
+        return k + 1, size, rho * rho, xi * (1.0 + rho)
+
+    begin = (jnp.int32(0), jnp.float32(1e30), jnp.max(rho0), jnp.max(inv_norm))
+    _, size, _, xi = lax.while_loop(more, body, begin)
     x = y_ref[...] + jnp.where(eye, xi, 0.0)
     rest = jnp.where(eye, 1.0, 0.0) - dot6(accs, c, x)
     sums_of([(rest.astype(BF16), [(square0, x.astype(BF16))])])
@@ -314,7 +311,7 @@
 
 def solve_kernel(
     plan, rows_all, near_ref, far_ref, sketch_ref, out_ref, log_ref,
-    packed, a_ref, x_ref, o_ref, y_ref, acc_ref,
+    packed, a_ref, x_ref, o_ref, y_ref, r1_ref, r2_ref, acc_ref,
     rows_ref, result, mats, parts, load_sem, store_sem,
 ):
     blocks = load_sem.shape[0]
@@ -356,7 +353,7 @@
         a_ref[rows(i), rows(i)] = mixed + unit
         a_ref[rows(j), rows(j)] = jnp.where(above, tile.T, tile) + unit
 
-    bufs = (o_ref, y_ref, acc_ref)
+    bufs = (o_ref, y_ref, r1_ref, r2_ref, acc_ref)
 
     def invert(*accs):
         x11, log1, size1 = near_inverse(accs, a_ref[:m, :m], *bufs)
@@ -448,7 +445,9 @@
             pltpu.VMEM((2 * plan.half, TILE), F32),
             pltpu.VMEM((width, width), F32),
             pltpu.VMEM((width, width), F32),
-            pltpu.VMEM((3, m, m), F32),
+            pltpu.VMEM((m, m), F32),
+            pltpu.VMEM((m, m), F32),
+            pltpu.VMEM((m, m), F32),
             pltpu.VMEM((m, m), F32),
             pltpu.VMEM((8, m), F32),
             pltpu.VMEM((rows, width), F32),

time: 247 us -> 247 us (level)
    ppermute x10 -> x11, waiting for transfers between devices: 16.1 us -> 15.5 us  [swap(): return lax.ppermute(x, AXES, [(i, i ^ mask) for i in range(self.n)])]
    ppermute x10 -> x11, starting transfers between devices: 12.9 us -> 13.1 us  [swap(): return lax.ppermute(x, AXES, [(i, i ^ mask) for i in range(self.n)])]
  transfers between devices with their start and end apart: 10 -> 11, of which waited for: 9 -> 10; matrix products, arithmetic and copies ran while one was open for 0% -> 0% of each run, Pallas kernels for 0% -> 0%
where the time goes in v2:
time: 247 us
  Pallas kernels  217 us (88%)
  waiting for transfers between devices  15.5 us (6%)
  starting transfers between devices  13.1 us (5%)
    pallas_call x1, Pallas kernels, solve(): pl.pallas_call(functools.partial(solve_kernel, plan, rows * plan.n), in_s...  210 us
    ppermute x11, waiting for transfers between devices, swap(): return lax.ppermute(x, AXES, [(i, i ^ mask) for i in range(self.n)])  15.5 us
    ppermute x11, starting transfers between devices, swap(): return lax.ppermute(x, AXES, [(i, i ^ mask) for i in range(self.n)])  13.1 us
    pallas_call x1, Pallas kernels, gram(): pl.pallas_call(functools.partial(gram_kernel, plan), in_specs=[pl.BlockSp...  7.12 us
  transfers between devices with their start and end apart: 11, of which 10 were waited for; matrix products, arithmetic and copies ran while one was open for 0% of the time, Pallas kernels for 0%

profile of v2, /device:TPU:0, one launch (start us, length us, event | category | flops | bytes accessed | tf_op | source)
XLA Modules:
  0.0 246.6 jit_solution(14678054557375646587)
XLA Ops:
  0.6 7.1 %shard_map.30 = (f32[544,128]{1,0:T(8,128)S(1)}, f32[544,128]{1,0:T(8,128)S(1)}) custom-call(f32[4096,512]{1,0:T(8,128)} %sketch_ref.3), custom_call_target="tpu_custom_call" | custom-call | tf_op jit(solution)/shard_map/pallas_call | solution.py:197
  7.8 0.5 collective-permute-start
  8.3 1.2 collective-permute-done
  9.5 2.9 %collective-permute-start.1 = (f32[136,128]{1,0:T(8,128)S(1)}, f32[136,128]{1,0:T(8,128)S(1)}, u32[]{:S(2)}, u32[]{:S(2)}) collective-permute-start(f32[136,128]{1,0:T(8,128)S(1)} %get-tuple-element.10), channel_id=1, source_target_pairs={{0,2},{1,3},{2,0},{3,1},{4,6},{5,7},{6,4},{7,5},{8,10},{9,11},{10,... | collective-permute-start | bytes 208904 | tf_op jit(solution)/shard_map/ppermute | solution.py:115
  12.5 1.4 collective-permute-start.3
  13.9 0.1 collective-permute-start.2
  14.0 1.8 collective-permute-done.1
  15.8 2.5 %collective-permute-done.3 = f32[136,128]{1,0:T(8,128)S(1)} collective-permute-done((f32[136,128]{1,0:T(8,128)S(1)}, f32[136,128]{1,0:T(8,128)S(1)}, u32[]{:S(2)}, u32[]{:S(2)}) %collective-permute-start.3) | collective-permute-done | bytes 69664 | tf_op jit(solution)/shard_map/ppermute | solution.py:115
  18.3 0.0 collective-permute-done.2
  18.4 3.7 %collective-permute-start.6 = (f32[136,128]{1,0:T(8,128)S(1)}, f32[136,128]{1,0:T(8,128)S(1)}, u32[]{:S(2)}, u32[]{:S(2)}) collective-permute-start(f32[136,128]{1,0:T(8,128)S(1)} %fusion.1), channel_id=1, source_target_pairs={{0,24},{1,25},{2,26},{3,27},{4,28},{5,29},{6,30},{7,31},{8,16},{9,... | collective-permute-start | bytes 208904 | tf_op jit(solution)/shard_map/ppermute | solution.py:115
  22.0 0.0 collective-permute-start.5
  22.0 0.8 collective-permute-start.4
  22.8 2.3 collective-permute-done.6
  25.1 2.4 collective-permute-done.5
  27.5 0.1 collective-permute-done.4
  27.6 1.9 collective-permute-start.9
  29.5 1.0 collective-permute-start.8
  30.6 0.6 collective-permute-start.7
  31.2 1.8 collective-permute-done.9
  33.0 0.8 collective-permute-done.8
  33.8 1.0 collective-permute-done.7
  34.9 0.1 collective-permute-start.10
  35.0 1.5 collective-permute-done.10.far_ref
  36.5 210.0 %shard_map.31 = (f32[4096,512]{1,0:T(8,128)}, f32[1,1]{1,0:T(1,128)}) custom-call(f32[544,128]{1,0:T(8,128)S(1)} %pad_maximum_fusion.near_ref, f32[544,128]{1,0:T(8,128)S(1)} %collective-permute-done.10.far_ref, f32[4096,512]{1,0:T(8,128)} %sketch_ref.3), custom_call_target="tpu_custom_call" | custom-call | tf_op jit(solution)/shard_map/pallas_call | solution.py:436
  (5 shorter events, 0.1 us)
Async XLA Ops:
  7.8 1.7 collective-permute-start
  9.5 6.3 %collective-permute-start.1 = (f32[136,128]{1,0:T(8,128)S(1)}, f32[136,128]{1,0:T(8,128)S(1)}, u32[]{:S(2)}, u32[]{:S(2)}) collective-permute-start(f32[136,128]{1,0:T(8,128)S(1)} %get-tuple-element.10), channel_id=1, source_target_pairs={{0,2},{1,3},{2,0},{3,1},{4,6},{5,7},{6,4},{7,5},{8,10},{9,11},{10,... | collective-permute-start | bytes 208904 | tf_op jit(solution)/shard_map/ppermute | solution.py:115
  12.5 5.9 %collective-permute-start.3 = (f32[136,128]{1,0:T(8,128)S(1)}, f32[136,128]{1,0:T(8,128)S(1)}, u32[]{:S(2)}, u32[]{:S(2)}) collective-permute-start(f32[136,128]{1,0:T(8,128)S(1)} %get-tuple-element.11), channel_id=1, source_target_pairs={{0,6},{1,7},{2,4},{3,5},{4,2},{5,3},{6,0},{7,1},{8,14},{9,15},{10,... | collective-permute-start | bytes 208904 | tf_op jit(solution)/shard_map/ppermute | solution.py:115
  13.9 4.4 %collective-permute-start.2 = (f32[136,128]{1,0:T(8,128)S(1)}, f32[136,128]{1,0:T(8,128)S(1)}, u32[]{:S(2)}, u32[]{:S(2)}) collective-permute-start(f32[136,128]{1,0:T(8,128)S(1)} %get-tuple-element.12), channel_id=1, source_target_pairs={{0,4},{1,5},{2,6},{3,7},{4,0},{5,1},{6,2},{7,3},{8,12},{9,13},{10,... | collective-permute-start | bytes 208904 | tf_op jit(solution)/shard_map/ppermute | solution.py:115
  18.4 6.7 %collective-permute-start.6 = (f32[136,128]{1,0:T(8,128)S(1)}, f32[136,128]{1,0:T(8,128)S(1)}, u32[]{:S(2)}, u32[]{:S(2)}) collective-permute-start(f32[136,128]{1,0:T(8,128)S(1)} %fusion.1), channel_id=1, source_target_pairs={{0,24},{1,25},{2,26},{3,27},{4,28},{5,29},{6,30},{7,31},{8,16},{9,... | collective-permute-start | bytes 208904 | tf_op jit(solution)/shard_map/ppermute | solution.py:115
  22.0 5.5 %collective-permute-start.5 = (f32[136,128]{1,0:T(8,128)S(1)}, f32[136,128]{1,0:T(8,128)S(1)}, u32[]{:S(2)}, u32[]{:S(2)}) collective-permute-start(f32[136,128]{1,0:T(8,128)S(1)} %fusion.1), channel_id=1, source_target_pairs={{0,16},{1,17},{2,18},{3,19},{4,20},{5,21},{6,22},{7,23},{8,24},{9,... | collective-permute-start | bytes 208904 | tf_op jit(solution)/shard_map/ppermute | solution.py:115
  22.0 5.6 %collective-permute-start.4 = (f32[136,128]{1,0:T(8,128)S(1)}, f32[136,128]{1,0:T(8,128)S(1)}, u32[]{:S(2)}, u32[]{:S(2)}) collective-permute-start(f32[136,128]{1,0:T(8,128)S(1)} %fusion.1), channel_id=1, source_target_pairs={{0,8},{1,9},{2,10},{3,11},{4,12},{5,13},{6,14},{7,15},{8,0},{9,1},... | collective-permute-start | bytes 208904 | tf_op jit(solution)/shard_map/ppermute | solution.py:115
  27.6 5.4 %collective-permute-start.9 = (f32[136,128]{1,0:T(8,128)S(1)}, f32[136,128]{1,0:T(8,128)S(1)}, u32[]{:S(2)}, u32[]{:S(2)}) collective-permute-start(f32[136,128]{1,0:T(8,128)S(1)} %add_add_fusion), channel_id=1, source_target_pairs={{0,6},{1,7},{2,4},{3,5},{4,2},{5,3},{6,0},{7,1},{8,14},{9,15},{10,... | collective-permute-start | bytes 208904 | tf_op jit(solution)/shard_map/ppermute | solution.py:115
  29.5 4.3 %collective-permute-start.8 = (f32[136,128]{1,0:T(8,128)S(1)}, f32[136,128]{1,0:T(8,128)S(1)}, u32[]{:S(2)}, u32[]{:S(2)}) collective-permute-start(f32[136,128]{1,0:T(8,128)S(1)} %add_add_fusion), channel_id=1, source_target_pairs={{0,4},{1,5},{2,6},{3,7},{4,0},{5,1},{6,2},{7,3},{8,12},{9,13},{10,... | collective-permute-start | bytes 208904 | tf_op jit(solution)/shard_map/ppermute | solution.py:115
  30.6 4.3 %collective-permute-start.7 = (f32[136,128]{1,0:T(8,128)S(1)}, f32[136,128]{1,0:T(8,128)S(1)}, u32[]{:S(2)}, u32[]{:S(2)}) collective-permute-start(f32[136,128]{1,0:T(8,128)S(1)} %add_add_fusion), channel_id=1, source_target_pairs={{0,2},{1,3},{2,0},{3,1},{4,6},{5,7},{6,4},{7,5},{8,10},{9,11},{10,... | collective-permute-start | bytes 208904 | tf_op jit(solution)/shard_map/ppermute | solution.py:115
  34.9 1.6 collective-permute-start.10

commit v3 on v2

--- a/solution.py
+++ b/solution.py
@@ -130,7 +130,9 @@
         return pltpu.make_async_copy(sketch_ref.at[at], rows_ref.at[at], load_sem.at[i])
 
     def prepare(i):
-        load(i).wait()
+        if i != 1 and i & (i - 1) == 0:
+            for j in range(i, min(max(2 * i, 2), blocks)):
+                load(j).wait()
         h, l = split(rows_ref[i * size : (i + 1) * size, :])
         flat[2 * (i % 2)] = h
         flat[2 * (i % 2) + 1] = l
@@ -220,9 +222,16 @@
     one, two = plan.z
     got = [plan.swap(own, z) for z in (one, two, one + two)]
     own = (own + got[0]) + (got[1] + got[2])
+    pieces = [own]
     for x, y in reversed(plan.stages):
-        own = jnp.concatenate([own] + [plan.swap(own, k) for k in (y, x, x + y)], axis=0)
-    return own, plan.swap(own, 1)
+        got = [plan.swap(piece, mask) for mask in (y, x, x + y) for piece in pieces]
+        pieces = pieces + got
+    far = [plan.swap(piece, 1) for piece in pieces]
+    return jnp.concatenate(pieces, axis=0), jnp.concatenate(far, axis=0)
+
+
+def log_near(x):
+    return jnp.where(x > 0.5, jnp.log1p(x - 1.0), jnp.log(x))
 
 
 def fold(x):
@@ -278,8 +287,8 @@
     rest = jnp.where(eye, 1.0, 0.0) - dot6(accs, c, x)
     sums_of([(rest.astype(BF16), [(square0, x.astype(BF16))])])
     x = x + pltpu.matmul_pop(square0)
-    log_det = n * jnp.log(norm) - jnp.sum(acc_ref[...], keepdims=True) - 2.0 * jnp.sum(
-        jnp.log(s_row), axis=1, keepdims=True
+    log_det = -n * log_near(inv_norm) - jnp.sum(acc_ref[...], keepdims=True) - 2.0 * jnp.sum(
+        log_near(s_row), axis=1, keepdims=True
     )
     return x * s_col * s_row, log_det, size
 
@@ -291,7 +300,7 @@
     s_row = lax.rsqrt(jnp.sum(diagonal, axis=0, keepdims=True))
     s_col = lax.rsqrt(jnp.sum(diagonal, axis=1, keepdims=True))
     c_ref[...] = a_ref[...] * s_col * s_row
-    log_ref[...] = -2.0 * jnp.sum(jnp.log(s_row), axis=1, keepdims=True)
+    log_ref[...] = -2.0 * jnp.sum(log_near(s_row), axis=1, keepdims=True)
     lane = lax.broadcasted_iota(jnp.int32, (1, n), 1)
 
     @pl.loop(0, n)
@@ -299,7 +308,7 @@
         row = c_ref[pl.ds(k, 1), :]
         here = lane == k
         pivot = jnp.sum(jnp.where(here, row, 0.0), axis=1, keepdims=True)
-        log_ref[...] += jnp.log(pivot)
+        log_ref[...] += log_near(pivot)
         u = jnp.where(here, pivot - 1.0, row)
         column = jnp.broadcast_to(u, (8, n)).T[:, :1]
         outer = column * (u / pivot)
@@ -399,6 +408,13 @@
             pltpu.matmul_push_rhs(tile, which, unit)
 
     def products(*accs):
+        def finish(i):
+            at = slice(i * size, (i + 1) * size)
+            for unit, acc in enumerate(accs[2 * (i % 2) : 2 * (i % 2) + 2]):
+                cols = slice(unit * m, (unit + 1) * m)
+                result[at, cols] = rows_ref[at, cols] * diagonal[:, cols] + pltpu.matmul_pop(acc)
+            store(i).start()
+
         push(0)
         push(1)
         prepare(0)
@@ -413,14 +429,11 @@
                     multiply(acc, parts[l, :, cols])
             if step + 2 < len(steps):
                 push(step + 2)
+            if k == 0 and which == 0 and i > 0:
+                finish(i - 1)
             if k == 0 and which == 1 and i + 1 < blocks:
                 prepare(i + 1)
-            if k == 1 and which == 1:
-                at = slice(i * size, (i + 1) * size)
-                for unit, acc in enumerate(mine):
-                    cols = slice(unit * m, (unit + 1) * m)
-                    result[at, cols] = rows_ref[at, cols] * diagonal[:, cols] + pltpu.matmul_pop(acc)
-                store(i).start()
+        finish(blocks - 1)
 
     pl.run_scoped(products, *[pltpu.ACC(unit)((size, m), F32) for unit in (0, 1, 0, 1)])
     for i in range(blocks):

time: 247 us -> 247 us (level)
    ppermute x11 -> x14, waiting for transfers between devices: 15.5 us -> 15.1 us  [swap(): return lax.ppermute(x, AXES, [(i, i ^ mask) for i in range(self.n)])]
    ppermute x11 -> x14, starting transfers between devices: 13.1 us -> 13 us  [swap(): return lax.ppermute(x, AXES, [(i, i ^ mask) for i in range(self.n)])]
  transfers between devices with their start and end apart: 11 -> 14, of which waited for: 10 -> 11; matrix products, arithmetic and copies ran while one was open for 0% -> 0% of each run, Pallas kernels for 0% -> 0%
where the time goes in v3:
time: 247 us
  Pallas kernels  218 us (88%)
  waiting for transfers between devices  15.1 us (6%)
  starting transfers between devices  13 us (5%)
    pallas_call x1, Pallas kernels, solve(): pl.pallas_call(functools.partial(solve_kernel, plan, rows * plan.n), in_s...  210 us
    ppermute x14, waiting for transfers between devices, swap(): return lax.ppermute(x, AXES, [(i, i ^ mask) for i in range(self.n)])  15.1 us
    ppermute x14, starting transfers between devices, swap(): return lax.ppermute(x, AXES, [(i, i ^ mask) for i in range(self.n)])  13 us
    pallas_call x1, Pallas kernels, gram(): pl.pallas_call(functools.partial(gram_kernel, plan), in_specs=[pl.BlockSp...  7.23 us
  transfers between devices with their start and end apart: 14, of which 11 were waited for; matrix products, arithmetic and copies ran while one was open for 0% of the time, Pallas kernels for 0%

profile of v3, /device:TPU:0, one launch (start us, length us, event | category | flops | bytes accessed | tf_op | source)
XLA Modules:
  0.0 246.6 jit_solution(496134099384355528)
XLA Ops:
  0.6 7.2 %shard_map.30 = (f32[544,128]{1,0:T(8,128)S(1)}, f32[544,128]{1,0:T(8,128)S(1)}) custom-call(f32[4096,512]{1,0:T(8,128)} %sketch_ref.3), custom_call_target="tpu_custom_call" | custom-call | tf_op jit(solution)/shard_map/pallas_call | solution.py:199
  7.9 0.5 collective-permute-start
  8.4 1.2 collective-permute-done
  9.6 3.0 %collective-permute-start.1 = (f32[136,128]{1,0:T(8,128)S(1)}, f32[136,128]{1,0:T(8,128)S(1)}, u32[]{:S(2)}, u32[]{:S(2)}) collective-permute-start(f32[136,128]{1,0:T(8,128)S(1)} %get-tuple-element.10), channel_id=1, source_target_pairs={{0,2},{1,3},{2,0},{3,1},{4,6},{5,7},{6,4},{7,5},{8,10},{9,11},{10,... | collective-permute-start | bytes 208904 | tf_op jit(solution)/shard_map/ppermute | solution.py:115
  12.6 1.4 collective-permute-start.3
  14.0 0.1 collective-permute-start.2
  14.1 1.8 collective-permute-done.1
  15.9 2.5 %collective-permute-done.3 = f32[136,128]{1,0:T(8,128)S(1)} collective-permute-done((f32[136,128]{1,0:T(8,128)S(1)}, f32[136,128]{1,0:T(8,128)S(1)}, u32[]{:S(2)}, u32[]{:S(2)}) %collective-permute-start.3) | collective-permute-done | bytes 69664 | tf_op jit(solution)/shard_map/ppermute | solution.py:115
  18.5 0.0 collective-permute-done.2
  18.5 3.6 %collective-permute-start.6 = (f32[136,128]{1,0:T(8,128)S(1)}, f32[136,128]{1,0:T(8,128)S(1)}, u32[]{:S(2)}, u32[]{:S(2)}) collective-permute-start(f32[136,128]{1,0:T(8,128)S(1)} %fusion.1), channel_id=1, source_target_pairs={{0,24},{1,25},{2,26},{3,27},{4,28},{5,29},{6,30},{7,31},{8,16},{9,... | collective-permute-start | bytes 208904 | tf_op jit(solution)/shard_map/ppermute | solution.py:115
  22.1 0.0 collective-permute-start.5
  22.1 0.8 collective-permute-start.4
  22.9 2.3 collective-permute-done.6
  25.2 2.4 collective-permute-done.5
  27.6 0.1 collective-permute-done.4
  27.7 1.9 collective-permute-start.9
  29.6 0.9 collective-permute-start.8
  30.6 0.7 collective-permute-start.7
  31.3 0.0 collective-permute-start.10
  31.3 1.8 collective-permute-done.9
  33.1 0.0 collective-permute-start.13
  33.1 0.8 collective-permute-done.8
  34.0 0.0 collective-permute-start.12
  34.0 0.9 collective-permute-done.7
  34.9 0.0 collective-permute-start.11
  34.9 0.0 collective-permute-done.10
  34.9 0.0 collective-permute-done.13
  34.9 0.3 collective-permute-done.12
  35.2 0.9 collective-permute-done.11
  36.2 210.3 %shard_map.31 = (f32[4096,512]{1,0:T(8,128)}, f32[1,1]{1,0:T(1,128)}) custom-call(f32[544,128]{1,0:T(8,128)S(1)} %pad_maximum_fusion.near_ref, f32[544,128]{1,0:T(8,128)S(1)} %pad_maximum_fusion.1.far_ref, f32[4096,512]{1,0:T(8,128)} %sketch_ref.3), custom_call_target="tpu_custom_call" | custom-call | tf_op jit(solution)/shard_map/pallas_call | solution.py:449
  (6 shorter events, 0.1 us)
Async XLA Ops:
  7.9 1.7 collective-permute-start
  9.6 6.3 %collective-permute-start.1 = (f32[136,128]{1,0:T(8,128)S(1)}, f32[136,128]{1,0:T(8,128)S(1)}, u32[]{:S(2)}, u32[]{:S(2)}) collective-permute-start(f32[136,128]{1,0:T(8,128)S(1)} %get-tuple-element.10), channel_id=1, source_target_pairs={{0,2},{1,3},{2,0},{3,1},{4,6},{5,7},{6,4},{7,5},{8,10},{9,11},{10,... | collective-permute-start | bytes 208904 | tf_op jit(solution)/shard_map/ppermute | solution.py:115
  12.6 5.9 %collective-permute-start.3 = (f32[136,128]{1,0:T(8,128)S(1)}, f32[136,128]{1,0:T(8,128)S(1)}, u32[]{:S(2)}, u32[]{:S(2)}) collective-permute-start(f32[136,128]{1,0:T(8,128)S(1)} %get-tuple-element.11), channel_id=1, source_target_pairs={{0,6},{1,7},{2,4},{3,5},{4,2},{5,3},{6,0},{7,1},{8,14},{9,15},{10,... | collective-permute-start | bytes 208904 | tf_op jit(solution)/shard_map/ppermute | solution.py:115
  14.0 4.4 %collective-permute-start.2 = (f32[136,128]{1,0:T(8,128)S(1)}, f32[136,128]{1,0:T(8,128)S(1)}, u32[]{:S(2)}, u32[]{:S(2)}) collective-permute-start(f32[136,128]{1,0:T(8,128)S(1)} %get-tuple-element.12), channel_id=1, source_target_pairs={{0,4},{1,5},{2,6},{3,7},{4,0},{5,1},{6,2},{7,3},{8,12},{9,13},{10,... | collective-permute-start | bytes 208904 | tf_op jit(solution)/shard_map/ppermute | solution.py:115
  18.5 6.7 %collective-permute-start.6 = (f32[136,128]{1,0:T(8,128)S(1)}, f32[136,128]{1,0:T(8,128)S(1)}, u32[]{:S(2)}, u32[]{:S(2)}) collective-permute-start(f32[136,128]{1,0:T(8,128)S(1)} %fusion.1), channel_id=1, source_target_pairs={{0,24},{1,25},{2,26},{3,27},{4,28},{5,29},{6,30},{7,31},{8,16},{9,... | collective-permute-start | bytes 208904 | tf_op jit(solution)/shard_map/ppermute | solution.py:115
  22.1 5.5 %collective-permute-start.5 = (f32[136,128]{1,0:T(8,128)S(1)}, f32[136,128]{1,0:T(8,128)S(1)}, u32[]{:S(2)}, u32[]{:S(2)}) collective-permute-start(f32[136,128]{1,0:T(8,128)S(1)} %fusion.1), channel_id=1, source_target_pairs={{0,16},{1,17},{2,18},{3,19},{4,20},{5,21},{6,22},{7,23},{8,24},{9,... | collective-permute-start | bytes 208904 | tf_op jit(solution)/shard_map/ppermute | solution.py:115
  22.1 5.6 %collective-permute-start.4 = (f32[136,128]{1,0:T(8,128)S(1)}, f32[136,128]{1,0:T(8,128)S(1)}, u32[]{:S(2)}, u32[]{:S(2)}) collective-permute-start(f32[136,128]{1,0:T(8,128)S(1)} %fusion.1), channel_id=1, source_target_pairs={{0,8},{1,9},{2,10},{3,11},{4,12},{5,13},{6,14},{7,15},{8,0},{9,1},... | collective-permute-start | bytes 208904 | tf_op jit(solution)/shard_map/ppermute | solution.py:115
  27.7 5.4 %collective-permute-start.9 = (f32[136,128]{1,0:T(8,128)S(1)}, f32[136,128]{1,0:T(8,128)S(1)}, u32[]{:S(2)}, u32[]{:S(2)}) collective-permute-start(f32[136,128]{1,0:T(8,128)S(1)} %add_add_fusion), channel_id=1, source_target_pairs={{0,6},{1,7},{2,4},{3,5},{4,2},{5,3},{6,0},{7,1},{8,14},{9,15},{10,... | collective-permute-start | bytes 208904 | tf_op jit(solution)/shard_map/ppermute | solution.py:115
  29.6 4.3 %collective-permute-start.8 = (f32[136,128]{1,0:T(8,128)S(1)}, f32[136,128]{1,0:T(8,128)S(1)}, u32[]{:S(2)}, u32[]{:S(2)}) collective-permute-start(f32[136,128]{1,0:T(8,128)S(1)} %add_add_fusion), channel_id=1, source_target_pairs={{0,4},{1,5},{2,6},{3,7},{4,0},{5,1},{6,2},{7,3},{8,12},{9,13},{10,... | collective-permute-start | bytes 208904 | tf_op jit(solution)/shard_map/ppermute | solution.py:115
  30.6 4.3 %collective-permute-start.7 = (f32[136,128]{1,0:T(8,128)S(1)}, f32[136,128]{1,0:T(8,128)S(1)}, u32[]{:S(2)}, u32[]{:S(2)}) collective-permute-start(f32[136,128]{1,0:T(8,128)S(1)} %add_add_fusion), channel_id=1, source_target_pairs={{0,2},{1,3},{2,0},{3,1},{4,6},{5,7},{6,4},{7,5},{8,10},{9,11},{10,... | collective-permute-start | bytes 208904 | tf_op jit(solution)/shard_map/ppermute | solution.py:115
  31.3 3.6 %collective-permute-start.10 = (f32[136,128]{1,0:T(8,128)S(1)}, f32[136,128]{1,0:T(8,128)S(1)}, u32[]{:S(2)}, u32[]{:S(2)}) collective-permute-start(f32[136,128]{1,0:T(8,128)S(1)} %add_add_fusion), channel_id=1, source_target_pairs={{0,1},{1,0},{2,3},{3,2},{4,5},{5,4},{6,7},{7,6},{8,9},{9,8},{10,11... | collective-permute-start | bytes 208904 | tf_op jit(solution)/shard_map/ppermute | solution.py:115
  33.1 1.8 collective-permute-start.13
  34.0 1.3 collective-permute-start.12
  34.9 1.3 collective-permute-start.11

commit v4 on v3

--- a/solution.py
+++ b/solution.py
@@ -214,11 +214,16 @@
 
 
 def share(plan, keep, send):
-    own = keep + plan.swap(send, 1)
+    own = None
     for x, y in plan.stages:
-        m = own.shape[0] // 4
-        got = [plan.swap(own[d * m : (d + 1) * m], k) for d, k in ((1, y), (2, x), (3, x + y))]
-        own = own[:m] + got[0] + got[1] + got[2]
+        m = (keep if own is None else own).shape[0] // 4
+        rows = [slice(d * m, (d + 1) * m) for d in range(4)]
+        if own is None:
+            cut = [keep[r] + plan.swap(send[r], 1) for r in rows]
+        else:
+            cut = [own[r] for r in rows]
+        got = [plan.swap(piece, mask) for piece, mask in zip(cut[1:], (y, x, x + y))]
+        own = cut[0] + got[0] + got[1] + got[2]
     one, two = plan.z
     got = [plan.swap(own, z) for z in (one, two, one + two)]
     own = (own + got[0]) + (got[1] + got[2])
@@ -228,10 +233,6 @@
         pieces = pieces + got
     far = [plan.swap(piece, 1) for piece in pieces]
     return jnp.concatenate(pieces, axis=0), jnp.concatenate(far, axis=0)
-
-
-def log_near(x):
-    return jnp.where(x > 0.5, jnp.log1p(x - 1.0), jnp.log(x))
 
 
 def fold(x):
@@ -287,8 +288,8 @@
     rest = jnp.where(eye, 1.0, 0.0) - dot6(accs, c, x)
     sums_of([(rest.astype(BF16), [(square0, x.astype(BF16))])])
     x = x + pltpu.matmul_pop(square0)
-    log_det = -n * log_near(inv_norm) - jnp.sum(acc_ref[...], keepdims=True) - 2.0 * jnp.sum(
-        log_near(s_row), axis=1, keepdims=True
+    log_det = n * jnp.log(norm) - jnp.sum(acc_ref[...], keepdims=True) - 2.0 * jnp.sum(
+        jnp.log(s_row), axis=1, keepdims=True
     )
     return x * s_col * s_row, log_det, size
 
@@ -300,7 +301,7 @@
     s_row = lax.rsqrt(jnp.sum(diagonal, axis=0, keepdims=True))
     s_col = lax.rsqrt(jnp.sum(diagonal, axis=1, keepdims=True))
     c_ref[...] = a_ref[...] * s_col * s_row
-    log_ref[...] = -2.0 * jnp.sum(log_near(s_row), axis=1, keepdims=True)
+    log_ref[...] = -2.0 * jnp.sum(jnp.log(s_row), axis=1, keepdims=True)
     lane = lax.broadcasted_iota(jnp.int32, (1, n), 1)
 
     @pl.loop(0, n)
@@ -308,7 +309,7 @@
         row = c_ref[pl.ds(k, 1), :]
         here = lane == k
         pivot = jnp.sum(jnp.where(here, row, 0.0), axis=1, keepdims=True)
-        log_ref[...] += log_near(pivot)
+        log_ref[...] += jnp.log(pivot)
         u = jnp.where(here, pivot - 1.0, row)
         column = jnp.broadcast_to(u, (8, n)).T[:, :1]
         outer = column * (u / pivot)

time: 247 us -> 247 us (level)
    ppermute x14 -> x17, starting transfers between devices: 13 us -> 13.6 us  [swap(): return lax.ppermute(x, AXES, [(i, i ^ mask) for i in range(self.n)])]
    ppermute x14 -> x17, waiting for transfers between devices: 15.1 us -> 14.7 us  [swap(): return lax.ppermute(x, AXES, [(i, i ^ mask) for i in range(self.n)])]
  transfers between devices with their start and end apart: 14 -> 17, of which waited for: 11 -> 13; matrix products, arithmetic and copies ran while one was open for 0% -> 0% of each run, Pallas kernels for 0% -> 0%
where the time goes in v4:
time: 247 us
  Pallas kernels  217 us (88%)
  waiting for transfers between devices  14.7 us (6%)
  starting transfers between devices  13.6 us (6%)
    pallas_call x1, Pallas kernels, solve(): pl.pallas_call(functools.partial(solve_kernel, plan, rows * plan.n), in_s...  210 us
    ppermute x17, waiting for transfers between devices, swap(): return lax.ppermute(x, AXES, [(i, i ^ mask) for i in range(self.n)])  14.7 us
    ppermute x17, starting transfers between devices, swap(): return lax.ppermute(x, AXES, [(i, i ^ mask) for i in range(self.n)])  13.6 us
    pallas_call x1, Pallas kernels, gram(): pl.pallas_call(functools.partial(gram_kernel, plan), in_specs=[pl.BlockSp...  7.23 us
  transfers between devices with their start and end apart: 17, of which 13 were waited for; matrix products, arithmetic and copies ran while one was open for 0% of the time, Pallas kernels for 0%

profile of v4, /device:TPU:0, one launch (start us, length us, event | category | flops | bytes accessed | tf_op | source)
XLA Modules:
  0.0 246.5 jit_solution(12349392063526618806)
XLA Ops:
  0.6 7.2 %shard_map.30 = (f32[544,128]{1,0:T(8,128)S(1)}, f32[544,128]{1,0:T(8,128)S(1)}) custom-call(f32[4096,512]{1,0:T(8,128)} %sketch_ref.3), custom_call_target="tpu_custom_call" | custom-call | tf_op jit(solution)/shard_map/pallas_call | solution.py:199
  7.9 0.5 collective-permute-start.5
  8.4 0.1 collective-permute-start.3
  8.5 0.4 collective-permute-start.1
  8.9 0.1 collective-permute-start
  9.0 0.3 collective-permute-done.5
  9.3 0.4 collective-permute-done.3
  9.7 0.2 collective-permute-done.1
  9.9 2.9 %collective-permute-start.2 = (f32[136,128]{1,0:T(8,128)S(1)}, f32[136,128]{1,0:T(8,128)S(1)}, u32[]{:S(2)}, u32[]{:S(2)}) collective-permute-start(f32[136,128]{1,0:T(8,128)S(1)} %get-tuple-element.14), channel_id=1, source_target_pairs={{0,2},{1,3},{2,0},{3,1},{4,6},{5,7},{6,4},{7,5},{8,10},{9,11},{10,... | collective-permute-start | bytes 208904 | tf_op jit(solution)/shard_map/ppermute | solution.py:115
  12.8 1.4 collective-permute-start.6
  14.2 0.1 collective-permute-start.4
  14.3 0.0 collective-permute-done
  14.3 1.8 collective-permute-done.2
  16.1 2.5 %collective-permute-done.6 = f32[136,128]{1,0:T(8,128)S(1)} collective-permute-done((f32[136,128]{1,0:T(8,128)S(1)}, f32[136,128]{1,0:T(8,128)S(1)}, u32[]{:S(2)}, u32[]{:S(2)}) %collective-permute-start.6) | collective-permute-done | bytes 69664 | tf_op jit(solution)/shard_map/ppermute | solution.py:115
  18.6 0.0 collective-permute-done.4
  18.7 3.6 %collective-permute-start.9 = (f32[136,128]{1,0:T(8,128)S(1)}, f32[136,128]{1,0:T(8,128)S(1)}, u32[]{:S(2)}, u32[]{:S(2)}) collective-permute-start(f32[136,128]{1,0:T(8,128)S(1)} %add_add_fusion.1), channel_id=1, source_target_pairs={{0,24},{1,25},{2,26},{3,27},{4,28},{5,29},{6,30},{7,31},{8,16},{9,... | collective-permute-start | bytes 208904 | tf_op jit(solution)/shard_map/ppermute | solution.py:115
  22.3 0.0 collective-permute-start.8
  22.3 0.8 collective-permute-start.7
  23.1 2.3 collective-permute-done.9
  25.4 2.4 collective-permute-done.8
  27.8 0.1 collective-permute-done.7
  27.9 2.0 collective-permute-start.12
  29.9 0.9 collective-permute-start.11
  30.8 0.7 collective-permute-start.10
  31.5 0.0 collective-permute-start.13
  31.5 1.8 collective-permute-done.12
  33.3 0.0 collective-permute-start.16
  33.3 0.9 collective-permute-done.11
  34.2 0.0 collective-permute-start.15
  34.2 0.9 collective-permute-done.10
  35.1 0.0 collective-permute-start.14
  35.1 0.0 collective-permute-done.13
  35.1 0.0 collective-permute-done.16
  35.1 0.3 collective-permute-done.15
  35.4 0.9 collective-permute-done.14
  36.4 210.0 %shard_map.31 = (f32[4096,512]{1,0:T(8,128)}, f32[1,1]{1,0:T(1,128)}) custom-call(f32[544,128]{1,0:T(8,128)S(1)} %pad_maximum_fusion.near_ref, f32[544,128]{1,0:T(8,128)S(1)} %pad_maximum_fusion.1.far_ref, f32[4096,512]{1,0:T(8,128)} %sketch_ref.3), custom_call_target="tpu_custom_call" | custom-call | tf_op jit(solution)/shard_map/pallas_call | solution.py:450
  (6 shorter events, 0.1 us)
Async XLA Ops:
  7.9 1.4 collective-permute-start.5
  8.4 1.3 collective-permute-start.3
  8.5 1.3 collective-permute-start.1
  8.9 5.4 %collective-permute-start = (f32[136,128]{1,0:T(8,128)S(1)}, f32[136,128]{1,0:T(8,128)S(1)}, u32[]{:S(2)}, u32[]{:S(2)}) collective-permute-start(f32[136,128]{1,0:T(8,128)S(1)} %get-tuple-element.10), channel_id=1, source_target_pairs={{0,1},{1,0},{2,3},{3,2},{4,5},{5,4},{6,7},{7,6},{8,9},{9,8},{10,11... | collective-permute-start | bytes 208904 | tf_op jit(solution)/shard_map/ppermute | solution.py:115
  9.9 6.3 %collective-permute-start.2 = (f32[136,128]{1,0:T(8,128)S(1)}, f32[136,128]{1,0:T(8,128)S(1)}, u32[]{:S(2)}, u32[]{:S(2)}) collective-permute-start(f32[136,128]{1,0:T(8,128)S(1)} %get-tuple-element.14), channel_id=1, source_target_pairs={{0,2},{1,3},{2,0},{3,1},{4,6},{5,7},{6,4},{7,5},{8,10},{9,11},{10,... | collective-permute-start | bytes 208904 | tf_op jit(solution)/shard_map/ppermute | solution.py:115
  12.8 5.8 %collective-permute-start.6 = (f32[136,128]{1,0:T(8,128)S(1)}, f32[136,128]{1,0:T(8,128)S(1)}, u32[]{:S(2)}, u32[]{:S(2)}) collective-permute-start(f32[136,128]{1,0:T(8,128)S(1)} %get-tuple-element.15), channel_id=1, source_target_pairs={{0,6},{1,7},{2,4},{3,5},{4,2},{5,3},{6,0},{7,1},{8,14},{9,15},{10,... | collective-permute-start | bytes 208904 | tf_op jit(solution)/shard_map/ppermute | solution.py:115
  14.2 4.4 %collective-permute-start.4 = (f32[136,128]{1,0:T(8,128)S(1)}, f32[136,128]{1,0:T(8,128)S(1)}, u32[]{:S(2)}, u32[]{:S(2)}) collective-permute-start(f32[136,128]{1,0:T(8,128)S(1)} %get-tuple-element.16), channel_id=1, source_target_pairs={{0,4},{1,5},{2,6},{3,7},{4,0},{5,1},{6,2},{7,3},{8,12},{9,13},{10,... | collective-permute-start | bytes 208904 | tf_op jit(solution)/shard_map/ppermute | solution.py:115
  18.7 6.7 %collective-permute-start.9 = (f32[136,128]{1,0:T(8,128)S(1)}, f32[136,128]{1,0:T(8,128)S(1)}, u32[]{:S(2)}, u32[]{:S(2)}) collective-permute-start(f32[136,128]{1,0:T(8,128)S(1)} %add_add_fusion.1), channel_id=1, source_target_pairs={{0,24},{1,25},{2,26},{3,27},{4,28},{5,29},{6,30},{7,31},{8,16},{9,... | collective-permute-start | bytes 208904 | tf_op jit(solution)/shard_map/ppermute | solution.py:115
  22.3 5.5 %collective-permute-start.8 = (f32[136,128]{1,0:T(8,128)S(1)}, f32[136,128]{1,0:T(8,128)S(1)}, u32[]{:S(2)}, u32[]{:S(2)}) collective-permute-start(f32[136,128]{1,0:T(8,128)S(1)} %add_add_fusion.1), channel_id=1, source_target_pairs={{0,16},{1,17},{2,18},{3,19},{4,20},{5,21},{6,22},{7,23},{8,24},{9,... | collective-permute-start | bytes 208904 | tf_op jit(solution)/shard_map/ppermute | solution.py:115
  22.3 5.6 %collective-permute-start.7 = (f32[136,128]{1,0:T(8,128)S(1)}, f32[136,128]{1,0:T(8,128)S(1)}, u32[]{:S(2)}, u32[]{:S(2)}) collective-permute-start(f32[136,128]{1,0:T(8,128)S(1)} %add_add_fusion.1), channel_id=1, source_target_pairs={{0,8},{1,9},{2,10},{3,11},{4,12},{5,13},{6,14},{7,15},{8,0},{9,1},... | collective-permute-start | bytes 208904 | tf_op jit(solution)/shard_map/ppermute | solution.py:115
  27.9 5.4 %collective-permute-start.12 = (f32[136,128]{1,0:T(8,128)S(1)}, f32[136,128]{1,0:T(8,128)S(1)}, u32[]{:S(2)}, u32[]{:S(2)}) collective-permute-start(f32[136,128]{1,0:T(8,128)S(1)} %add_add_fusion), channel_id=1, source_target_pairs={{0,6},{1,7},{2,4},{3,5},{4,2},{5,3},{6,0},{7,1},{8,14},{9,15},{10,... | collective-permute-start | bytes 208904 | tf_op jit(solution)/shard_map/ppermute | solution.py:115
  29.9 4.3 %collective-permute-start.11 = (f32[136,128]{1,0:T(8,128)S(1)}, f32[136,128]{1,0:T(8,128)S(1)}, u32[]{:S(2)}, u32[]{:S(2)}) collective-permute-start(f32[136,128]{1,0:T(8,128)S(1)} %add_add_fusion), channel_id=1, source_target_pairs={{0,4},{1,5},{2,6},{3,7},{4,0},{5,1},{6,2},{7,3},{8,12},{9,13},{10,... | collective-permute-start | bytes 208904 | tf_op jit(solution)/shard_map/ppermute | solution.py:115
  30.8 4.3 %collective-permute-start.10 = (f32[136,128]{1,0:T(8,128)S(1)}, f32[136,128]{1,0:T(8,128)S(1)}, u32[]{:S(2)}, u32[]{:S(2)}) collective-permute-start(f32[136,128]{1,0:T(8,128)S(1)} %add_add_fusion), channel_id=1, source_target_pairs={{0,2},{1,3},{2,0},{3,1},{4,6},{5,7},{6,4},{7,5},{8,10},{9,11},{10,... | collective-permute-start | bytes 208904 | tf_op jit(solution)/shard_map/ppermute | solution.py:115
  31.5 3.6 %collective-permute-start.13 = (f32[136,128]{1,0:T(8,128)S(1)}, f32[136,128]{1,0:T(8,128)S(1)}, u32[]{:S(2)}, u32[]{:S(2)}) collective-permute-start(f32[136,128]{1,0:T(8,128)S(1)} %add_add_fusion), channel_id=1, source_target_pairs={{0,1},{1,0},{2,3},{3,2},{4,5},{5,4},{6,7},{7,6},{8,9},{9,8},{10,11... | collective-permute-start | bytes 208904 | tf_op jit(solution)/shard_map/ppermute | solution.py:115
  33.3 1.8 collective-permute-start.16
  34.2 1.3 collective-permute-start.15
  35.1 1.3 collective-permute-start.14

commit v5 on v3

--- a/solution.py
+++ b/solution.py
@@ -228,10 +228,6 @@
         pieces = pieces + got
     far = [plan.swap(piece, 1) for piece in pieces]
     return jnp.concatenate(pieces, axis=0), jnp.concatenate(far, axis=0)
-
-
-def log_near(x):
-    return jnp.where(x > 0.5, jnp.log1p(x - 1.0), jnp.log(x))
 
 
 def fold(x):
@@ -287,8 +283,8 @@
     rest = jnp.where(eye, 1.0, 0.0) - dot6(accs, c, x)
     sums_of([(rest.astype(BF16), [(square0, x.astype(BF16))])])
     x = x + pltpu.matmul_pop(square0)
-    log_det = -n * log_near(inv_norm) - jnp.sum(acc_ref[...], keepdims=True) - 2.0 * jnp.sum(
-        log_near(s_row), axis=1, keepdims=True
+    log_det = n * jnp.log(norm) - jnp.sum(acc_ref[...], keepdims=True) - 2.0 * jnp.sum(
+        jnp.log(s_row), axis=1, keepdims=True
     )
     return x * s_col * s_row, log_det, size
 
@@ -300,7 +296,7 @@
     s_row = lax.rsqrt(jnp.sum(diagonal, axis=0, keepdims=True))
     s_col = lax.rsqrt(jnp.sum(diagonal, axis=1, keepdims=True))
     c_ref[...] = a_ref[...] * s_col * s_row
-    log_ref[...] = -2.0 * jnp.sum(log_near(s_row), axis=1, keepdims=True)
+    log_ref[...] = -2.0 * jnp.sum(jnp.log(s_row), axis=1, keepdims=True)
     lane = lax.broadcasted_iota(jnp.int32, (1, n), 1)
 
     @pl.loop(0, n)
@@ -308,7 +304,7 @@
         row = c_ref[pl.ds(k, 1), :]
         here = lane == k
         pivot = jnp.sum(jnp.where(here, row, 0.0), axis=1, keepdims=True)
-        log_ref[...] += log_near(pivot)
+        log_ref[...] += jnp.log(pivot)
         u = jnp.where(here, pivot - 1.0, row)
         column = jnp.broadcast_to(u, (8, n)).T[:, :1]
         outer = column * (u / pivot)

time: 247 us -> 246 us (level)
  no operation moved by 1% of the time
where the time goes in v5:
time: 246 us
  Pallas kernels  217 us (88%)
  waiting for transfers between devices  15.1 us (6%)
  starting transfers between devices  13 us (5%)
    pallas_call x1, Pallas kernels, solve(): pl.pallas_call(functools.partial(solve_kernel, plan, rows * plan.n), in_s...  210 us
    ppermute x14, waiting for transfers between devices, swap(): return lax.ppermute(x, AXES, [(i, i ^ mask) for i in range(self.n)])  15.1 us
    ppermute x14, starting transfers between devices, swap(): return lax.ppermute(x, AXES, [(i, i ^ mask) for i in range(self.n)])  13 us
    pallas_call x1, Pallas kernels, gram(): pl.pallas_call(functools.partial(gram_kernel, plan), in_specs=[pl.BlockSp...  7.23 us
  transfers between devices with their start and end apart: 14, of which 11 were waited for; matrix products, arithmetic and copies ran while one was open for 0% of the time, Pallas kernels for 0%

profile of v5, /device:TPU:0, one launch (start us, length us, event | category | flops | bytes accessed | tf_op | source)
XLA Modules:
  0.0 246.3 jit_solution(18369304417685472975)
XLA Ops:
  0.6 7.2 %shard_map.30 = (f32[544,128]{1,0:T(8,128)S(1)}, f32[544,128]{1,0:T(8,128)S(1)}) custom-call(f32[4096,512]{1,0:T(8,128)} %sketch_ref.3), custom_call_target="tpu_custom_call" | custom-call | tf_op jit(solution)/shard_map/pallas_call | solution.py:199
  7.9 0.5 collective-permute-start
  8.4 1.2 collective-permute-done
  9.6 3.0 %collective-permute-start.1 = (f32[136,128]{1,0:T(8,128)S(1)}, f32[136,128]{1,0:T(8,128)S(1)}, u32[]{:S(2)}, u32[]{:S(2)}) collective-permute-start(f32[136,128]{1,0:T(8,128)S(1)} %get-tuple-element.10), channel_id=1, source_target_pairs={{0,2},{1,3},{2,0},{3,1},{4,6},{5,7},{6,4},{7,5},{8,10},{9,11},{10,... | collective-permute-start | bytes 208904 | tf_op jit(solution)/shard_map/ppermute | solution.py:115
  12.6 1.4 collective-permute-start.3
  14.0 0.1 collective-permute-start.2
  14.1 1.8 collective-permute-done.1
  15.9 2.5 %collective-permute-done.3 = f32[136,128]{1,0:T(8,128)S(1)} collective-permute-done((f32[136,128]{1,0:T(8,128)S(1)}, f32[136,128]{1,0:T(8,128)S(1)}, u32[]{:S(2)}, u32[]{:S(2)}) %collective-permute-start.3) | collective-permute-done | bytes 69664 | tf_op jit(solution)/shard_map/ppermute | solution.py:115
  18.5 0.0 collective-permute-done.2
  18.5 3.6 %collective-permute-start.6 = (f32[136,128]{1,0:T(8,128)S(1)}, f32[136,128]{1,0:T(8,128)S(1)}, u32[]{:S(2)}, u32[]{:S(2)}) collective-permute-start(f32[136,128]{1,0:T(8,128)S(1)} %fusion.1), channel_id=1, source_target_pairs={{0,24},{1,25},{2,26},{3,27},{4,28},{5,29},{6,30},{7,31},{8,16},{9,... | collective-permute-start | bytes 208904 | tf_op jit(solution)/shard_map/ppermute | solution.py:115
  22.1 0.0 collective-permute-start.5
  22.1 0.8 collective-permute-start.4
  22.9 2.3 collective-permute-done.6
  25.2 2.4 collective-permute-done.5
  27.6 0.1 collective-permute-done.4
  27.7 1.9 collective-permute-start.9
  29.6 0.9 collective-permute-start.8
  30.6 0.7 collective-permute-start.7
  31.3 0.0 collective-permute-start.10
  31.3 1.8 collective-permute-done.9
  33.1 0.0 collective-permute-start.13
  33.1 0.8 collective-permute-done.8
  34.0 0.0 collective-permute-start.12
  34.0 0.9 collective-permute-done.7
  34.9 0.0 collective-permute-start.11
  34.9 0.0 collective-permute-done.10
  34.9 0.0 collective-permute-done.13
  34.9 0.3 collective-permute-done.12
  35.2 0.9 collective-permute-done.11
  36.2 210.0 %shard_map.31 = (f32[4096,512]{1,0:T(8,128)}, f32[1,1]{1,0:T(1,128)}) custom-call(f32[544,128]{1,0:T(8,128)S(1)} %pad_maximum_fusion.near_ref, f32[544,128]{1,0:T(8,128)S(1)} %pad_maximum_fusion.1.far_ref, f32[4096,512]{1,0:T(8,128)} %sketch_ref.3), custom_call_target="tpu_custom_call" | custom-call | tf_op jit(solution)/shard_map/pallas_call | solution.py:445
  (6 shorter events, 0.1 us)
Async XLA Ops:
  7.9 1.7 collective-permute-start
  9.6 6.3 %collective-permute-start.1 = (f32[136,128]{1,0:T(8,128)S(1)}, f32[136,128]{1,0:T(8,128)S(1)}, u32[]{:S(2)}, u32[]{:S(2)}) collective-permute-start(f32[136,128]{1,0:T(8,128)S(1)} %get-tuple-element.10), channel_id=1, source_target_pairs={{0,2},{1,3},{2,0},{3,1},{4,6},{5,7},{6,4},{7,5},{8,10},{9,11},{10,... | collective-permute-start | bytes 208904 | tf_op jit(solution)/shard_map/ppermute | solution.py:115
  12.6 5.9 %collective-permute-start.3 = (f32[136,128]{1,0:T(8,128)S(1)}, f32[136,128]{1,0:T(8,128)S(1)}, u32[]{:S(2)}, u32[]{:S(2)}) collective-permute-start(f32[136,128]{1,0:T(8,128)S(1)} %get-tuple-element.11), channel_id=1, source_target_pairs={{0,6},{1,7},{2,4},{3,5},{4,2},{5,3},{6,0},{7,1},{8,14},{9,15},{10,... | collective-permute-start | bytes 208904 | tf_op jit(solution)/shard_map/ppermute | solution.py:115
  14.0 4.4 %collective-permute-start.2 = (f32[136,128]{1,0:T(8,128)S(1)}, f32[136,128]{1,0:T(8,128)S(1)}, u32[]{:S(2)}, u32[]{:S(2)}) collective-permute-start(f32[136,128]{1,0:T(8,128)S(1)} %get-tuple-element.12), channel_id=1, source_target_pairs={{0,4},{1,5},{2,6},{3,7},{4,0},{5,1},{6,2},{7,3},{8,12},{9,13},{10,... | collective-permute-start | bytes 208904 | tf_op jit(solution)/shard_map/ppermute | solution.py:115
  18.5 6.7 %collective-permute-start.6 = (f32[136,128]{1,0:T(8,128)S(1)}, f32[136,128]{1,0:T(8,128)S(1)}, u32[]{:S(2)}, u32[]{:S(2)}) collective-permute-start(f32[136,128]{1,0:T(8,128)S(1)} %fusion.1), channel_id=1, source_target_pairs={{0,24},{1,25},{2,26},{3,27},{4,28},{5,29},{6,30},{7,31},{8,16},{9,... | collective-permute-start | bytes 208904 | tf_op jit(solution)/shard_map/ppermute | solution.py:115
  22.1 5.5 %collective-permute-start.5 = (f32[136,128]{1,0:T(8,128)S(1)}, f32[136,128]{1,0:T(8,128)S(1)}, u32[]{:S(2)}, u32[]{:S(2)}) collective-permute-start(f32[136,128]{1,0:T(8,128)S(1)} %fusion.1), channel_id=1, source_target_pairs={{0,16},{1,17},{2,18},{3,19},{4,20},{5,21},{6,22},{7,23},{8,24},{9,... | collective-permute-start | bytes 208904 | tf_op jit(solution)/shard_map/ppermute | solution.py:115
  22.1 5.6 %collective-permute-start.4 = (f32[136,128]{1,0:T(8,128)S(1)}, f32[136,128]{1,0:T(8,128)S(1)}, u32[]{:S(2)}, u32[]{:S(2)}) collective-permute-start(f32[136,128]{1,0:T(8,128)S(1)} %fusion.1), channel_id=1, source_target_pairs={{0,8},{1,9},{2,10},{3,11},{4,12},{5,13},{6,14},{7,15},{8,0},{9,1},... | collective-permute-start | bytes 208904 | tf_op jit(solution)/shard_map/ppermute | solution.py:115
  27.7 5.4 %collective-permute-start.9 = (f32[136,128]{1,0:T(8,128)S(1)}, f32[136,128]{1,0:T(8,128)S(1)}, u32[]{:S(2)}, u32[]{:S(2)}) collective-permute-start(f32[136,128]{1,0:T(8,128)S(1)} %add_add_fusion), channel_id=1, source_target_pairs={{0,6},{1,7},{2,4},{3,5},{4,2},{5,3},{6,0},{7,1},{8,14},{9,15},{10,... | collective-permute-start | bytes 208904 | tf_op jit(solution)/shard_map/ppermute | solution.py:115
  29.6 4.3 %collective-permute-start.8 = (f32[136,128]{1,0:T(8,128)S(1)}, f32[136,128]{1,0:T(8,128)S(1)}, u32[]{:S(2)}, u32[]{:S(2)}) collective-permute-start(f32[136,128]{1,0:T(8,128)S(1)} %add_add_fusion), channel_id=1, source_target_pairs={{0,4},{1,5},{2,6},{3,7},{4,0},{5,1},{6,2},{7,3},{8,12},{9,13},{10,... | collective-permute-start | bytes 208904 | tf_op jit(solution)/shard_map/ppermute | solution.py:115
  30.6 4.3 %collective-permute-start.7 = (f32[136,128]{1,0:T(8,128)S(1)}, f32[136,128]{1,0:T(8,128)S(1)}, u32[]{:S(2)}, u32[]{:S(2)}) collective-permute-start(f32[136,128]{1,0:T(8,128)S(1)} %add_add_fusion), channel_id=1, source_target_pairs={{0,2},{1,3},{2,0},{3,1},{4,6},{5,7},{6,4},{7,5},{8,10},{9,11},{10,... | collective-permute-start | bytes 208904 | tf_op jit(solution)/shard_map/ppermute | solution.py:115
  31.3 3.6 %collective-permute-start.10 = (f32[136,128]{1,0:T(8,128)S(1)}, f32[136,128]{1,0:T(8,128)S(1)}, u32[]{:S(2)}, u32[]{:S(2)}) collective-permute-start(f32[136,128]{1,0:T(8,128)S(1)} %add_add_fusion), channel_id=1, source_target_pairs={{0,1},{1,0},{2,3},{3,2},{4,5},{5,4},{6,7},{7,6},{8,9},{9,8},{10,11... | collective-permute-start | bytes 208904 | tf_op jit(solution)/shard_map/ppermute | solution.py:115
  33.1 1.8 collective-permute-start.13
  34.0 1.3 collective-permute-start.12
  34.9 1.3 collective-permute-start.11

commit v6 on v5

--- a/solution.py
+++ b/solution.py
@@ -374,7 +374,8 @@
         x_ref[m:, :m] = x12.T
         x_ref[m:, m:] = x22
         log_ref[...] = log1 + log2
-        good = jnp.logical_and(size1 < 1e-3, size2 < 1e-3)
+        lost = jnp.max(jnp.sum(jnp.where(eye_mask(m), a_ref[m:, m:] - 32.0 * schur, 0.0), axis=0))
+        good = jnp.logical_and(jnp.logical_and(size1 < 1e-3, size2 < 1e-3), lost <= 0.0)
 
         @pl.when(jnp.logical_not(good))
         def _():

time: 246 us -> 246 us (level)
  no operation moved by 1% of the time
where the time goes in v6:
time: 246 us
  Pallas kernels  217 us (88%)
  waiting for transfers between devices  15.1 us (6%)
  starting transfers between devices  13 us (5%)
    pallas_call x1, Pallas kernels, solve(): pl.pallas_call(functools.partial(solve_kernel, plan, rows * plan.n), in_s...  210 us
    ppermute x14, waiting for transfers between devices, swap(): return lax.ppermute(x, AXES, [(i, i ^ mask) for i in range(self.n)])  15.1 us
    ppermute x14, starting transfers between devices, swap(): return lax.ppermute(x, AXES, [(i, i ^ mask) for i in range(self.n)])  13 us
    pallas_call x1, Pallas kernels, gram(): pl.pallas_call(functools.partial(gram_kernel, plan), in_specs=[pl.BlockSp...  7.23 us
  transfers between devices with their start and end apart: 14, of which 11 were waited for; matrix products, arithmetic and copies ran while one was open for 0% of the time, Pallas kernels for 0%

profile of v6, /device:TPU:0, one launch (start us, length us, event | category | flops | bytes accessed | tf_op | source)
XLA Modules:
  0.0 246.3 jit_solution(6855851580019501577)
XLA Ops:
  0.6 7.2 %shard_map.30 = (f32[544,128]{1,0:T(8,128)S(1)}, f32[544,128]{1,0:T(8,128)S(1)}) custom-call(f32[4096,512]{1,0:T(8,128)} %sketch_ref.3), custom_call_target="tpu_custom_call" | custom-call | tf_op jit(solution)/shard_map/pallas_call | solution.py:199
  7.9 0.5 collective-permute-start
  8.4 1.2 collective-permute-done
  9.6 3.0 %collective-permute-start.1 = (f32[136,128]{1,0:T(8,128)S(1)}, f32[136,128]{1,0:T(8,128)S(1)}, u32[]{:S(2)}, u32[]{:S(2)}) collective-permute-start(f32[136,128]{1,0:T(8,128)S(1)} %get-tuple-element.10), channel_id=1, source_target_pairs={{0,2},{1,3},{2,0},{3,1},{4,6},{5,7},{6,4},{7,5},{8,10},{9,11},{10,... | collective-permute-start | bytes 208904 | tf_op jit(solution)/shard_map/ppermute | solution.py:115
  12.6 1.4 collective-permute-start.3
  14.0 0.1 collective-permute-start.2
  14.1 1.8 collective-permute-done.1
  15.9 2.5 %collective-permute-done.3 = f32[136,128]{1,0:T(8,128)S(1)} collective-permute-done((f32[136,128]{1,0:T(8,128)S(1)}, f32[136,128]{1,0:T(8,128)S(1)}, u32[]{:S(2)}, u32[]{:S(2)}) %collective-permute-start.3) | collective-permute-done | bytes 69664 | tf_op jit(solution)/shard_map/ppermute | solution.py:115
  18.5 0.0 collective-permute-done.2
  18.5 3.6 %collective-permute-start.6 = (f32[136,128]{1,0:T(8,128)S(1)}, f32[136,128]{1,0:T(8,128)S(1)}, u32[]{:S(2)}, u32[]{:S(2)}) collective-permute-start(f32[136,128]{1,0:T(8,128)S(1)} %fusion.1), channel_id=1, source_target_pairs={{0,24},{1,25},{2,26},{3,27},{4,28},{5,29},{6,30},{7,31},{8,16},{9,... | collective-permute-start | bytes 208904 | tf_op jit(solution)/shard_map/ppermute | solution.py:115
  22.1 0.0 collective-permute-start.5
  22.1 0.8 collective-permute-start.4
  22.9 2.3 collective-permute-done.6
  25.2 2.4 collective-permute-done.5
  27.6 0.1 collective-permute-done.4
  27.7 1.9 collective-permute-start.9
  29.6 0.9 collective-permute-start.8
  30.6 0.7 collective-permute-start.7
  31.3 0.0 collective-permute-start.10
  31.3 1.8 collective-permute-done.9
  33.1 0.0 collective-permute-start.13
  33.1 0.8 collective-permute-done.8
  34.0 0.0 collective-permute-start.12
  34.0 0.9 collective-permute-done.7
  34.9 0.0 collective-permute-start.11
  34.9 0.0 collective-permute-done.10
  34.9 0.0 collective-permute-done.13
  34.9 0.3 collective-permute-done.12
  35.2 0.9 collective-permute-done.11
  36.2 210.0 %shard_map.31 = (f32[4096,512]{1,0:T(8,128)}, f32[1,1]{1,0:T(1,128)}) custom-call(f32[544,128]{1,0:T(8,128)S(1)} %pad_maximum_fusion.near_ref, f32[544,128]{1,0:T(8,128)S(1)} %pad_maximum_fusion.1.far_ref, f32[4096,512]{1,0:T(8,128)} %sketch_ref.3), custom_call_target="tpu_custom_call" | custom-call | tf_op jit(solution)/shard_map/pallas_call | solution.py:446
  (6 shorter events, 0.1 us)
Async XLA Ops:
  7.9 1.7 collective-permute-start
  9.6 6.3 %collective-permute-start.1 = (f32[136,128]{1,0:T(8,128)S(1)}, f32[136,128]{1,0:T(8,128)S(1)}, u32[]{:S(2)}, u32[]{:S(2)}) collective-permute-start(f32[136,128]{1,0:T(8,128)S(1)} %get-tuple-element.10), channel_id=1, source_target_pairs={{0,2},{1,3},{2,0},{3,1},{4,6},{5,7},{6,4},{7,5},{8,10},{9,11},{10,... | collective-permute-start | bytes 208904 | tf_op jit(solution)/shard_map/ppermute | solution.py:115
  12.6 5.9 %collective-permute-start.3 = (f32[136,128]{1,0:T(8,128)S(1)}, f32[136,128]{1,0:T(8,128)S(1)}, u32[]{:S(2)}, u32[]{:S(2)}) collective-permute-start(f32[136,128]{1,0:T(8,128)S(1)} %get-tuple-element.11), channel_id=1, source_target_pairs={{0,6},{1,7},{2,4},{3,5},{4,2},{5,3},{6,0},{7,1},{8,14},{9,15},{10,... | collective-permute-start | bytes 208904 | tf_op jit(solution)/shard_map/ppermute | solution.py:115
  14.0 4.4 %collective-permute-start.2 = (f32[136,128]{1,0:T(8,128)S(1)}, f32[136,128]{1,0:T(8,128)S(1)}, u32[]{:S(2)}, u32[]{:S(2)}) collective-permute-start(f32[136,128]{1,0:T(8,128)S(1)} %get-tuple-element.12), channel_id=1, source_target_pairs={{0,4},{1,5},{2,6},{3,7},{4,0},{5,1},{6,2},{7,3},{8,12},{9,13},{10,... | collective-permute-start | bytes 208904 | tf_op jit(solution)/shard_map/ppermute | solution.py:115
  18.5 6.7 %collective-permute-start.6 = (f32[136,128]{1,0:T(8,128)S(1)}, f32[136,128]{1,0:T(8,128)S(1)}, u32[]{:S(2)}, u32[]{:S(2)}) collective-permute-start(f32[136,128]{1,0:T(8,128)S(1)} %fusion.1), channel_id=1, source_target_pairs={{0,24},{1,25},{2,26},{3,27},{4,28},{5,29},{6,30},{7,31},{8,16},{9,... | collective-permute-start | bytes 208904 | tf_op jit(solution)/shard_map/ppermute | solution.py:115
  22.1 5.5 %collective-permute-start.5 = (f32[136,128]{1,0:T(8,128)S(1)}, f32[136,128]{1,0:T(8,128)S(1)}, u32[]{:S(2)}, u32[]{:S(2)}) collective-permute-start(f32[136,128]{1,0:T(8,128)S(1)} %fusion.1), channel_id=1, source_target_pairs={{0,16},{1,17},{2,18},{3,19},{4,20},{5,21},{6,22},{7,23},{8,24},{9,... | collective-permute-start | bytes 208904 | tf_op jit(solution)/shard_map/ppermute | solution.py:115
  22.1 5.6 %collective-permute-start.4 = (f32[136,128]{1,0:T(8,128)S(1)}, f32[136,128]{1,0:T(8,128)S(1)}, u32[]{:S(2)}, u32[]{:S(2)}) collective-permute-start(f32[136,128]{1,0:T(8,128)S(1)} %fusion.1), channel_id=1, source_target_pairs={{0,8},{1,9},{2,10},{3,11},{4,12},{5,13},{6,14},{7,15},{8,0},{9,1},... | collective-permute-start | bytes 208904 | tf_op jit(solution)/shard_map/ppermute | solution.py:115
  27.7 5.4 %collective-permute-start.9 = (f32[136,128]{1,0:T(8,128)S(1)}, f32[136,128]{1,0:T(8,128)S(1)}, u32[]{:S(2)}, u32[]{:S(2)}) collective-permute-start(f32[136,128]{1,0:T(8,128)S(1)} %add_add_fusion), channel_id=1, source_target_pairs={{0,6},{1,7},{2,4},{3,5},{4,2},{5,3},{6,0},{7,1},{8,14},{9,15},{10,... | collective-permute-start | bytes 208904 | tf_op jit(solution)/shard_map/ppermute | solution.py:115
  29.6 4.3 %collective-permute-start.8 = (f32[136,128]{1,0:T(8,128)S(1)}, f32[136,128]{1,0:T(8,128)S(1)}, u32[]{:S(2)}, u32[]{:S(2)}) collective-permute-start(f32[136,128]{1,0:T(8,128)S(1)} %add_add_fusion), channel_id=1, source_target_pairs={{0,4},{1,5},{2,6},{3,7},{4,0},{5,1},{6,2},{7,3},{8,12},{9,13},{10,... | collective-permute-start | bytes 208904 | tf_op jit(solution)/shard_map/ppermute | solution.py:115
  30.6 4.3 %collective-permute-start.7 = (f32[136,128]{1,0:T(8,128)S(1)}, f32[136,128]{1,0:T(8,128)S(1)}, u32[]{:S(2)}, u32[]{:S(2)}) collective-permute-start(f32[136,128]{1,0:T(8,128)S(1)} %add_add_fusion), channel_id=1, source_target_pairs={{0,2},{1,3},{2,0},{3,1},{4,6},{5,7},{6,4},{7,5},{8,10},{9,11},{10,... | collective-permute-start | bytes 208904 | tf_op jit(solution)/shard_map/ppermute | solution.py:115
  31.3 3.6 %collective-permute-start.10 = (f32[136,128]{1,0:T(8,128)S(1)}, f32[136,128]{1,0:T(8,128)S(1)}, u32[]{:S(2)}, u32[]{:S(2)}) collective-permute-start(f32[136,128]{1,0:T(8,128)S(1)} %add_add_fusion), channel_id=1, source_target_pairs={{0,1},{1,0},{2,3},{3,2},{4,5},{5,4},{6,7},{7,6},{8,9},{9,8},{10,11... | collective-permute-start | bytes 208904 | tf_op jit(solution)/shard_map/ppermute | solution.py:115
  33.1 1.8 collective-permute-start.13
  34.0 1.3 collective-permute-start.12
  34.9 1.3 collective-permute-start.11
